TPU v7x, 512 devices: a whole 4x8x8 slice. The times are simulated.
512 devices in a mesh: ent: 64 (over z, y), rel: 8 (over x, core).
Axes of the slice: x: 4, y: 8, z: 8, core: 2. Of those that a mesh axis runs over, the one named last changes fastest.
Arguments:
- features: bfloat16 [16384, 256], P('ent'), may hold values from -6 to 6
- basis_stack: bfloat16 [64, 256, 256], P('rel'), may hold values from -0.375 to 0.375
- coeffs: float32 [1300, 64], P(None, 'rel'), may hold values from -0.75 to 0.75
- self_weight: bfloat16 [256, 256], P(None, 'rel'), may hold values from -0.375 to 0.375
- src_row: int32 [4096, 32], P('ent'), may hold values from 0 to 255
- dst_row: int32 [4096, 32], P('ent'), may hold values from 0 to 255
- rel_id: int32 [4096, 32], P('ent'), may hold values from 0 to 1299
- edge_weight: float32 [4096, 32], P('ent'), may hold values from 0.05 to 1
- counts: int32 [64, 64], P('ent'), may hold values from 1 to 32, as said below
- out_grad: bfloat16 [16384, 256], P('ent', 'rel'), may hold values from -6 to 6
Outputs:
- layer_out: bfloat16 [16384, 256], P('ent', 'rel')
- input_grad: float32 [16384, 256], P('ent', 'rel')
- coef_grad: float32 [1300, 64], P(None, 'rel')
- basis_grad: float32 [64, 256, 256], P('rel')
- self_grad: float32 [256, 256], P(None, 'rel')
Inputs may be any that keep to these rules, and one draw needn't show every extreme that they name: Slots at or beyond counts[s, d] are padding. Some destination shard receives 32 live slots from every source shard.
All inputs are finite; a program needn't handle non-finite values.
Results may differ from a plain program's by a relative error of at most 0.013.
Values may be sent and summed in bfloat16 or wider, within the bound.
No kernel may reach another device: no remote copies, remote signals or barrier semaphores. Data moves between devices by JAX's collectives and lax.ppermute only.
A program may use at most 64 MiB of HBM per device.

v0:
```python
import jax
import jax.numpy as jnp
from jax import lax
from jax.sharding import PartitionSpec as P


def body(
    features,
    basis_stack,
    coeffs,
    self_weight,
    src_row,
    dst_row,
    rel_id,
    edge_weight,
    counts,
    out_grad,
):
    row_count = features.shape[0]
    width = features.shape[1]
    shards = src_row.shape[0]
    slot_count = src_row.shape[1]
    relations = coeffs.shape[0]
    live_slot = (jnp.arange(slot_count, dtype=jnp.int32)[None, :] < counts[0][:, None]).astype(
        jnp.float32
    )
    slot_weight = (edge_weight * live_slot).reshape(-1)
    src_flat = src_row.reshape(-1)
    dst_flat = dst_row.reshape(-1)
    rel_flat = rel_id.reshape(-1)
    zvals = jnp.einsum(
        "ui,bio->ubo", features, basis_stack, preferred_element_type=jnp.float32
    ).astype(jnp.bfloat16)
    gathered = jnp.take(zvals, src_flat, axis=0)
    coef_edge = jnp.take(coeffs, rel_flat, axis=0)
    mixed = jnp.einsum("eb,ebd->ed", coef_edge, gathered.astype(jnp.float32))
    partial_value = (
        (slot_weight[:, None] * mixed).astype(jnp.bfloat16).reshape(shards, slot_count, width)
    )
    self_term = jnp.dot(features, self_weight, preferred_element_type=jnp.float32)
    received = lax.all_to_all(partial_value, "ent", split_axis=0, concat_axis=0, tiled=True)
    local_sum = jax.ops.segment_sum(
        received.reshape(-1, width).astype(jnp.float32), dst_flat, num_segments=row_count
    )
    summed = lax.psum_scatter(local_sum, "rel", scatter_dimension=1, tiled=True)
    preact = summed + self_term
    sigmoid_pre = jax.nn.sigmoid(preact)
    layer_out = (preact * sigmoid_pre).astype(jnp.bfloat16)
    grad_pre = (
        out_grad.astype(jnp.float32) * sigmoid_pre * (1.0 + preact * (1.0 - sigmoid_pre))
    ).astype(jnp.bfloat16)
    grad_full = lax.all_gather(grad_pre, "rel", axis=1, tiled=True)
    grad_slot = jnp.take(grad_full, dst_flat, axis=0).reshape(shards, slot_count, width)
    grad_msg = lax.all_to_all(grad_slot, "ent", split_axis=0, concat_axis=0, tiled=True)
    grad_msg = grad_msg.reshape(-1, width)
    inner_prod = jnp.einsum("ebd,ed->eb", gathered, grad_msg, preferred_element_type=jnp.float32)
    coef_local = jax.ops.segment_sum(
        inner_prod * slot_weight[:, None], rel_flat, num_segments=relations
    )
    scaled = (slot_weight[:, None] * coef_edge)[:, :, None] * grad_msg.astype(jnp.float32)[
        :, None, :
    ]
    grad_z = jax.ops.segment_sum(scaled, src_flat, num_segments=row_count).astype(jnp.bfloat16)
    basis_local = jnp.einsum("ui,ubo->bio", features, grad_z, preferred_element_type=jnp.float32)
    self_local = jnp.dot(features.T, grad_pre, preferred_element_type=jnp.float32)
    coef_grad, basis_grad, self_grad = lax.psum((coef_local, basis_local, self_local), "ent")
    input_local = jnp.einsum("ubo,bio->ui", grad_z, basis_stack, preferred_element_type=jnp.float32)
    input_local = input_local + jnp.dot(grad_pre, self_weight.T, preferred_element_type=jnp.float32)
    input_grad = lax.psum_scatter(input_local, "rel", scatter_dimension=1, tiled=True)
    return (layer_out, input_grad, coef_grad, basis_grad, self_grad)


def solution(mesh):
    return jax.shard_map(
        body,
        mesh=mesh,
        in_specs=(
            P("ent", None),
            P("rel", None, None),
            P(None, "rel"),
            P(None, "rel"),
            P("ent", None),
            P("ent", None),
            P("ent", None),
            P("ent", None),
            P("ent", None),
            P("ent", "rel"),
        ),
        out_specs=(
            P("ent", "rel"),
            P("ent", "rel"),
            P(None, "rel"),
            P("rel", None, None),
            P(None, "rel"),
        ),
        check_vma=False,
    )
```

profile of v0, /device:TPU:56, one launch (start us, length us, event | category | flops | bytes accessed | tf_op | source)
XLA Modules:
  0.0 768.4 jit_solution(5026522460678729545)
XLA Ops:
  13.2 7.6 gather_fusion
  20.8 15.7 %gather_fusion.1 = bf16[2048,8,256]{2,1,0:T(8,128)(2,1)} fusion(bf16[256,8,256]{2,1,0:T(8,128)(2,1)S(1)} %copy.29, s32[2048]{0:T(1024)S(1)} %broadcast_clamp_fusion.1), kind=kCustom, calls=%fused_computation.1 | custom fusion | bytes 16785408 | tf_op jit(solution)/shard_map/jit(_take)/gather | solution.py:34
  36.5 1.7 broadcast_multiply_fusion.1
  38.2 9.2 %fusion.1 = f32[2048,1,256]{2,1,0:T(1,128)S(1)} fusion(f32[2048,8,1]{1,2,0:T(1,128)S(1)} %bitcast.47, bf16[2048,8,256]{2,1,0:T(8,128)(2,1)} %gather_fusion.1, pred[2048]{0:T(1024)(128)(4,1)S(1)} %compare_and_fusion.1), kind=kOutput, calls=%fused_computation.9 | convolution fusion | flops 12582912 | bytes 10553344 | tf_op jit(solution)/shard_map/eb,ebd->ed/dot_general | solution.py:36
  48.7 16.0 %all-to-all-start = ((bf16[64,32,256]{2,1,0:T(8,128)(2,1)}), bf16[64,32,256]{2,1,0:T(8,128)(2,1)S(1)}, u32[]{:S(2)}, u32[]{:S(2)}) async-start(bf16[64,32,256]{2,1,0:T(8,128)(2,1)} %bitcast.7), calls=%async_computation | async-start | bytes 2097152 | tf_op jit(solution)/shard_map/all_to_all | solution.py:41
  65.2 28.3 %all-to-all-done = bf16[64,32,256]{2,1,0:T(8,128)(2,1)S(1)} async-done(((bf16[64,32,256]{2,1,0:T(8,128)(2,1)}), bf16[64,32,256]{2,1,0:T(8,128)(2,1)S(1)}, u32[]{:S(2)}, u32[]{:S(2)}) %all-to-all-start) | async-done | bytes 1048608 | tf_op jit(solution)/shard_map/all_to_all | solution.py:41
  93.5 12.3 %scatter_custom_fusion = f32[256,256]{1,0:T(8,128)} fusion(s32[2048]{0:T(1024)S(1)} %reshape.212, bf16[2048,256]{1,0:T(8,128)(2,1)S(1)} %bitcast.44, f32[]{:T(128)} %constant.31.clone.1), kind=kCustom, calls=%fused_computation.10 | custom fusion | flops 1048576 | bytes 1310724 | tf_op jit(solution)/shard_map/scatter-add | solution.py:42
  105.8 1.8 copy.30
  107.7 31.5 %reduce-scatter.3.cloned.1.call-done = f32[256,32]{0,1:T(8,128)} async-done(((f32[256,256]{0,1:T(8,128)}), f32[256,32]{0,1:T(8,128)}) %reduce-scatter.3.cloned.1.call-update) | async-done | bytes 32784 | tf_op jit(solution)/shard_map/reduce_scatter | solution.py:45
  140.8 12.7 %all_gather.3 = bf16[256,256]{0,1:T(8,128)(2,1)S(1)} all-gather(bf16[256,32]{0,1:T(8,128)(2,1)S(1)} %get-tuple-element.19), channel_id=1, replica_groups=mesh['ent'=64,'rel'=8] {'rel'}, dimensions={1}, use_global_device_ids=true | all-gather | bytes 147456 | tf_op jit(solution)/shard_map/all_gather | solution.py:52
  153.6 7.5 gather_fusion.2
  162.3 13.2 %all-to-all-start.1 = ((bf16[64,32,256]{2,1,0:T(8,128)(2,1)}), bf16[64,32,256]{2,1,0:T(8,128)(2,1)S(1)}, u32[]{:S(2)}, u32[]{:S(2)}) async-start(bf16[64,32,256]{2,1,0:T(8,128)(2,1)} %broadcast_select_fusion.3), calls=%async_computation.2 | async-start | bytes 2097152 | tf_op jit(solution)/shard_map/all_to_all | solution.py:54
  176.6 28.3 %all-to-all-done.1 = bf16[64,32,256]{2,1,0:T(8,128)(2,1)S(1)} async-done(((bf16[64,32,256]{2,1,0:T(8,128)(2,1)}), bf16[64,32,256]{2,1,0:T(8,128)(2,1)S(1)}, u32[]{:S(2)}, u32[]{:S(2)}) %all-to-all-start.1) | async-done | bytes 1048608 | tf_op jit(solution)/shard_map/all_to_all | solution.py:54
  204.9 17.9 %fusion = f32[2048,1,8]{2,1,0:T(1,128)} fusion(bf16[2048,8,256]{2,1,0:T(8,128)(2,1)} %gather_fusion.1, pred[2048]{0:T(1024)(128)(4,1)S(1)} %compare_and_fusion.1, bf16[2048,256,1]{1,0,2:T(8,128)(2,1)S(1)} %bitcast.43), kind=kOutput, calls=%fused_computation.8 | convolution fusion | flops 12582912 | bytes 9504768 | tf_op jit(solution)/shard_map/ebd,ed->eb/dot_general | solution.py:56
  222.7 13.7 %scatter_custom_fusion.2 = f32[1300,8]{1,0:T(8,128)} fusion(s32[2048]{0:T(1024)S(1)} %reshape.179, f32[2048,8]{1,0:T(8,128)} %bitcast.46, f32[2048]{0:T(1024)S(1)} %mul.57, f32[]{:T(128)} %constant.31.clone.1), kind=kCustom, calls=%fused_computation.22 | custom fusion | flops 32768 | bytes 115332 | tf_op jit(solution)/shard_map/scatter-add | solution.py:57
  236.7 9.4 %broadcast_multiply_fusion = f32[2048,8,256]{2,1,0:T(8,128)} fusion(f32[2048,256]{1,0:T(8,128)S(1)} %bitcast_convert_fusion, f32[2048,8]{1,0:T(8,128)S(1)} %get-tuple-element.17), kind=kLoop, calls=%fused_computation.6 | loop fusion | flops 4194304 | bytes 18939904 | tf_op jit(solution)/shard_map/mul | solution.py:60
  246.2 158.8 %scatter_fusion = f32[256,8,256]{2,1,0:T(8,128)S(1)} fusion(f32[256,8,256]{2,1,0:T(8,128)S(1)} %broadcast_in_dim.47, s32[2048]{0:T(1024)S(1)} %reshape.181, f32[2048,8,256]{2,1,0:T(8,128)} %broadcast_multiply_fusion), kind=kCustom, calls=%fused_computation.4 | custom fusion | flops 4194304 | bytes 50339840 | tf_op jit(solution)/shard_map/scatter-add | solution.py:63
  406.1 1.6 copy.35
  407.8 1.7 convolution_bitcast_fusion
  411.0 149.4 %all-reduce.6.cloned.1.call-done = (f32[1300,8]{1,0:T(8,128)}, f32[256,32]{0,1:T(8,128)}) async-done(((f32[1300,8]{1,0:T(8,128)}, f32[256,32]{0,1:T(8,128)}), (f32[1300,8]{1,0:T(8,128)}, f32[256,32]{0,1:T(8,128)})) %all-reduce.6.cloned.1.call-update) | async-done | bytes 74384 | tf_op jit(solution)/shard_map/psum | solution.py:66
  560.5 1.9 copy.36
  562.4 162.2 %all-reduce.4.cloned.1.call-done = f32[8,256,256]{1,2,0:T(8,128)} async-done(((f32[8,256,256]{1,2,0:T(8,128)}), f32[8,256,256]{1,2,0:T(8,128)}) %all-reduce.4.cloned.1.call-update) | async-done | bytes 2097168 | tf_op jit(solution)/shard_map/psum | solution.py:66
  724.6 2.9 copy.37
  727.5 33.8 %reduce-scatter.5.cloned.1.call-done = f32[256,32]{0,1:T(8,128)} async-done(((f32[256,256]{0,1:T(8,128)}), f32[256,32]{0,1:T(8,128)}) %reduce-scatter.5.cloned.1.call-update) | async-done | bytes 32784 | tf_op jit(solution)/shard_map/reduce_scatter | solution.py:69
  (56 shorter events, 15.1 us)
Async XLA Ops:
  7.2 4.0 copy-start
  47.4 17.4 %copy-start.2 = (s32[64,32]{0,1:T(8,128)S(1)}, s32[64,32]{0,1:T(8,128)}, u32[]{:S(2)}) copy-start(s32[64,32]{0,1:T(8,128)} %param.15) | copy-start | bytes 24580
  48.7 90.5 %copy-start.1 = (bf16[256,256]{1,0:T(8,128)(2,1)S(1)}, bf16[256,256]{1,0:T(8,128)(2,1)}, u32[]{:S(2)}) copy-start(bf16[256,256]{1,0:T(8,128)(2,1)} %param.10) | copy-start | bytes 393220
  48.7 90.5 %copy-start.4 = (bf16[256,32]{0,1:T(8,128)(2,1)S(1)}, bf16[256,32]{0,1:T(8,128)(2,1)}, u32[]{:S(2)}) copy-start(bf16[256,32]{0,1:T(8,128)(2,1)} %param.13) | copy-start | bytes 49156
  48.7 90.5 %copy-start.5 = (bf16[256,32]{0,1:T(8,128)(2,1)S(1)}, bf16[256,32]{0,1:T(8,128)(2,1)}, u32[]{:S(2)}) copy-start(bf16[256,32]{0,1:T(8,128)(2,1)} %param.19) | copy-start | bytes 49156
  48.7 44.8 %all-to-all-start = ((bf16[64,32,256]{2,1,0:T(8,128)(2,1)}), bf16[64,32,256]{2,1,0:T(8,128)(2,1)S(1)}, u32[]{:S(2)}, u32[]{:S(2)}) async-start(bf16[64,32,256]{2,1,0:T(8,128)(2,1)} %bitcast.7), calls=%async_computation | async-start | bytes 2097152 | tf_op jit(solution)/shard_map/all_to_all | solution.py:41
  64.8 74.4 %reduce-scatter.3.cloned.1.call-start = ((), (), s32[]{:S(2)}) async-start(), calls=%async_computation.4 | async-start | bytes 294912 | tf_op jit(solution)/shard_map/reduce_scatter | solution.py:45
  162.3 42.5 %all-to-all-start.1 = ((bf16[64,32,256]{2,1,0:T(8,128)(2,1)}), bf16[64,32,256]{2,1,0:T(8,128)(2,1)S(1)}, u32[]{:S(2)}, u32[]{:S(2)}) async-start(bf16[64,32,256]{2,1,0:T(8,128)(2,1)} %broadcast_select_fusion.3), calls=%async_computation.2 | async-start | bytes 2097152 | tf_op jit(solution)/shard_map/all_to_all | solution.py:54
  175.6 384.9 %all-reduce.6.cloned.1.call-start = ((), (), s32[]{:S(2)}) async-start(), calls=%async_computation.7 | async-start | bytes 1400832 | tf_op jit(solution)/shard_map/psum | solution.py:66
  407.7 316.9 %all-reduce.4.cloned.1.call-start = ((), (), s32[]{:S(2)}) async-start(), calls=%async_computation.6 | async-start | bytes 4194304 | tf_op jit(solution)/shard_map/psum | solution.py:66
  409.5 351.7 %reduce-scatter.5.cloned.1.call-start = ((), (), s32[]{:S(2)}) async-start(), calls=%async_computation.5 | async-start | bytes 294912 | tf_op jit(solution)/shard_map/reduce_scatter | solution.py:69
  562.4 198.9 %copy-start.3 = (f32[256,32]{0,1:T(8,128)S(1)}, f32[256,32]{0,1:T(8,128)}, u32[]{:S(2)}) copy-start(f32[256,32]{0,1:T(8,128)} %get-tuple-element.25) | copy-start | bytes 98308
Sparse Core Ops, SparseCore 0:
  107.8 31.3 reduce-scatter.2
  407.8 152.5 all-reduce.5
  564.6 159.9 all-reduce.3
  728.1 33.1 reduce-scatter.4
where the time goes:
time: 772 us; the launch traced here: 768 us
  waiting for transfers between devices  434 us (56%)
  other arithmetic  201 us (26%)
  local copies, waits for them, and re-layouts  44.1 us (6%)
  matrix products  33.8 us (4%)
  starting transfers between devices  29.6 us (4%)
  between operations  14 us (2%)
  blocking collectives  12.7 us (2%)
    psum x2, waiting for transfers between devices, body(): lax.psum((coef_local, basis_local, self_local), 'ent')  312 us
    scatter-add x1, other arithmetic, body(): jax.ops.segment_sum(scaled, src_flat, num_segments=row_count)  159 us
    reduce_scatter x1, waiting for transfers between devices, body(): lax.psum_scatter(input_local, 'rel', scatter_dimension=1, tiled=True)  33.8 us
    reduce_scatter x1, waiting for transfers between devices, body(): summed = lax.psum_scatter(local_sum, 'rel', scatter_dimension=1, tiled=True)  31.5 us
    all_to_all x1, waiting for transfers between devices, body(): lax.all_to_all(partial_value, 'ent', split_axis=0, concat_axis=0, tiled=T...  28.3 us
    all_to_all x1, waiting for transfers between devices, body(): lax.all_to_all(grad_slot, 'ent', split_axis=0, concat_axis=0, tiled=True)  28.3 us
    dot_general x1, matrix products, body(): jnp.einsum('ebd,ed->eb', gathered, grad_msg, preferred_element_type=jnp.f...  17.9 us
    all_to_all x1, starting transfers between devices, body(): lax.all_to_all(partial_value, 'ent', split_axis=0, concat_axis=0, tiled=T...  16 us
  transfers between devices with their start and end apart: 6, of which 6 were waited for; matrix products, arithmetic and copies ran while one was open for 1% of the time, Pallas kernels for 0%

commit v1 on v0

v1 whole, which is shorter than its diff:
```python
import jax
import jax.numpy as jnp
from jax import lax
from jax.experimental import pallas as pl
from jax.experimental.pallas import tpu as pltpu
from jax.sharding import PartitionSpec as P


F32 = jnp.float32
BF16 = jnp.bfloat16

D = 256
NE = 64
NK = 8
GB = 8
COL = 32
RELS = 1300
REL_CHUNK = 24
REL_PAD = 1344
REL_LANES = 1536
SLOTS = 2048
BLK = 256
W_ROWS = 304
G_ROWS = 80
X_ROWS = 96


def nn(a, b):
    return lax.dot_general(a, b, (((1,), (0,)), ((), ())), preferred_element_type=F32)


def nt(a, b):
    return lax.dot_general(a, b, (((1,), (1,)), ((), ())), preferred_element_type=F32)


def tn(a, b):
    return lax.dot_general(a, b, (((0,), (0,)), ((), ())), preferred_element_type=F32)


def hot(rows, index):
    place = lax.broadcasted_iota(jnp.int32, (rows, index.shape[1]), 0)
    return jnp.where(place == index, 1.0, 0.0).astype(BF16)


def call(kernel, out_shape, scratch=(), smem=0, flops=0):
    def run(*args):
        specs = [
            pl.BlockSpec(memory_space=pltpu.SMEM if n < smem else pltpu.VMEM)
            for n in range(len(args))
        ]
        return pl.pallas_call(
            kernel,
            out_shape=out_shape,
            in_specs=specs,
            out_specs=jax.tree.map(lambda _: pl.BlockSpec(memory_space=pltpu.VMEM), out_shape),
            scratch_shapes=list(scratch),
            compiler_params=pltpu.CompilerParams(vmem_limit_bytes=48 * 1024 * 1024),
            cost_estimate=pl.CostEstimate(flops=flops, bytes_accessed=4 << 20, transcendentals=0),
        )(*args)

    return run


def share_kernel(basis_ref, coef_ref, out_ref, pad_ref):
    pad_ref[...] = jnp.zeros_like(pad_ref)
    pad_ref[:, 0:RELS] = coef_ref[...]
    for l in range(GB):
        turned = basis_ref[l].astype(F32).T.astype(BF16)
        for k in range(NK):
            out_ref[k, l * COL : (l + 1) * COL, :] = turned[k * COL : (k + 1) * COL, :]
    for t in range(3):
        pair = jnp.concatenate(
            [pad_ref[:, t * 512 : t * 512 + 256], pad_ref[:, t * 512 + 256 : t * 512 + 512]], axis=0
        ).astype(BF16)
        for k in range(NK):
            out_ref[k, 256 + t * 16 : 256 + t * 16 + 16, :] = pair


def message_kernel(w_ref, x_ref, index_ref, weight_ref, out_ref, coef_ref, coef_all, z_ref, msg_ref):
    for g in range(NK):
        for t in range(3):
            pair = w_ref[g, 256 + t * 16 : 256 + t * 16 + 16, :].astype(F32)
            coef_all[g * GB : (g + 1) * GB, t * 512 : t * 512 + 256] = pair[0:8]
            coef_all[g * GB : (g + 1) * GB, t * 512 + 256 : t * 512 + 512] = pair[8:16]
        z_ref[g * 256 : (g + 1) * 256, :] = nt(w_ref[g, 0:256, :], x_ref[...]).astype(BF16)
    coef_table = coef_all[:, 0:REL_PAD].astype(BF16)

    def block(step, carry):
        lanes = pl.ds(pl.multiple_of(step * BLK, BLK), BLK)
        source = hot(256, index_ref[0:1, lanes])
        coef_ref[:, lanes] = nn(coef_table, hot(REL_PAD, index_ref[2:3, lanes]))
        total = jnp.zeros((COL, BLK), F32)
        for g in range(NK):
            taken = nn(z_ref[g * 256 : (g + 1) * 256, :], source)
            for l in range(GB):
                total += coef_ref[pl.ds(g * GB + l, 1), lanes] * taken[l * COL : (l + 1) * COL, :]
        rows = pl.ds(pl.multiple_of((step // 2) * COL, COL), COL)
        part = pl.ds(pl.multiple_of((step % 2) * BLK, BLK), BLK)
        msg_ref[rows, part] = total * weight_ref[0:1, lanes]
        return carry

    lax.fori_loop(0, SLOTS // BLK, block, 0)
    out_ref[...] = msg_ref[...].T.astype(BF16)


def node_kernel(got_ref, index_ref, x_ref, self_ref, out_grad_ref, out_ref, layer_ref, grad_ref, msg_ref):
    arrived = got_ref[...].astype(F32).T.astype(BF16)
    pre = nt(self_ref[...], x_ref[...])
    for q in range(4):
        lanes = slice(q * 512, (q + 1) * 512)
        pre += nt(arrived[q * COL : (q + 1) * COL, :], hot(256, index_ref[1:2, lanes]))
    sig = jax.nn.sigmoid(pre)
    layer_ref[...] = (pre * sig).astype(BF16)
    grad = (out_grad_ref[...].astype(F32) * sig * (1.0 + pre * (1.0 - sig))).astype(BF16)
    grad_ref[...] = grad
    for q in range(4):
        lanes = slice(q * 512, (q + 1) * 512)
        msg_ref[q * COL : (q + 1) * COL, :] = nn(grad, hot(256, index_ref[1:2, lanes]))
    out_ref[...] = msg_ref[...].T.astype(BF16)


def grad_kernel(
    got_ref,
    w_ref,
    coef_ref,
    x_ref,
    index_ref,
    weight_ref,
    self_ref,
    grad_ref,
    out_ref,
    input_ref,
    z_ref,
    m_ref,
    src_ref,
    rel_ref,
    scaled_ref,
    inner_ref,
):
    x = x_ref[...]
    for g in range(NK):
        z_ref[g * 256 : (g + 1) * 256, :] = nt(w_ref[g, 0:256, :], x).astype(BF16)
    arrived = got_ref[...].astype(F32).T
    for q in range(4):
        m_ref[:, q * 512 : (q + 1) * 512] = arrived[q * COL : (q + 1) * COL, :]

    def block(step, carry):
        lanes = pl.ds(pl.multiple_of(step * BLK, BLK), BLK)
        source = hot(256, index_ref[0:1, lanes])
        src_ref[:, lanes] = source
        rel_ref[:, lanes] = hot(REL_PAD, index_ref[2:3, lanes])
        m = m_ref[:, lanes]
        weighted = m * weight_ref[0:1, lanes]
        for g in range(NK):
            taken = nn(z_ref[g * 256 : (g + 1) * 256, :], source)
            for l in range(GB):
                b = g * GB + l
                inner_ref[b : b + 1, lanes] = jnp.sum(
                    taken[l * COL : (l + 1) * COL, :] * weighted, axis=0, keepdims=True
                )
                scaled_ref[b * COL : (b + 1) * COL, lanes] = (
                    coef_ref[pl.ds(b, 1), lanes] * weighted
                ).astype(BF16)
        return carry

    lax.fori_loop(0, SLOTS // BLK, block, 0)

    turned = x.astype(F32).T.astype(BF16)
    total = tn(grad_ref[...], self_ref[...])
    for pair in range(NK // 2):
        terms = []
        for g in (2 * pair, 2 * pair + 1):
            grad_z = nt(src_ref[...], scaled_ref[g * 256 : (g + 1) * 256, :]).astype(BF16)
            total += nn(grad_z, w_ref[g, 0:256, :])
            terms.append(nn(turned, grad_z))
        for h in range(2):
            for ib in range(32):
                rows, lanes = slice(ib * 8, ib * 8 + 8), slice(h * 128, h * 128 + 128)
                out_ref[h * 32 + ib, pair * 16 : pair * 16 + 16, :] = jnp.concatenate(
                    [terms[0][rows, lanes], terms[1][rows, lanes]], axis=0
                ).astype(BF16)
    input_ref[...] = total.T.astype(BF16)

    coef = nt(rel_ref[...], inner_ref[...].astype(BF16))
    own = nt(turned, grad_ref[...])
    for n in range(NE):
        low = jnp.zeros((16, 64), F32)
        third = jnp.zeros((8, 64), F32)
        if (n + 1) * REL_CHUNK <= REL_PAD:
            low = coef[n * REL_CHUNK : n * REL_CHUNK + 16, :]
            third = coef[n * REL_CHUNK + 16 : n * REL_CHUNK + 24, :]
        rest = jnp.zeros((8, 64), F32)
        if n < 32:
            rest = jnp.concatenate([own[n * 8 : n * 8 + 8, :], jnp.zeros((8, 32), F32)], axis=1)
        high = jnp.concatenate([third, rest], axis=0)
        out_ref[n, 64:80, :] = jnp.concatenate([low, high], axis=1).astype(BF16)


def sum_kernel(got_ref, input_ref, out_ref, own_ref):
    def add(n, total):
        return total + got_ref[n].astype(F32)

    total = lax.fori_loop(0, NE, add, jnp.zeros((G_ROWS, 128), F32), unroll=8)
    own_ref[...] = total[72:80]
    for k in range(NK):
        rows = slice(k * COL, (k + 1) * COL)
        out_ref[k, 0:32, :] = input_ref[rows, 0:128]
        out_ref[k, 32:64, :] = input_ref[rows, 128:256]
        out_ref[k, 64:80, :] = jnp.concatenate([total[k * 8 : k * 8 + 8], total[64:72]], axis=0).astype(BF16)
        out_ref[k, 80:96, :] = jnp.concatenate([total[72:80], jnp.zeros((8, 128), F32)], axis=0).astype(BF16)


def merge_kernel(me_ref, got_ref, own_ref, out_ref, input_ref):
    me = me_ref[0]
    total = got_ref[0, 0:64, :].astype(F32)
    slab = got_ref[0, 64:96, :].astype(F32)
    pieces = [slab[0:8]]
    for k in range(1, NK):
        total += got_ref[k, 0:64, :].astype(F32)
        more = got_ref[k, 64:96, :].astype(F32)
        pieces.append(more[0:8])
        slab = slab + more
    input_ref[:, 0:128] = total[0:32]
    input_ref[:, 128:256] = total[32:64]
    lane = lax.broadcasted_iota(jnp.int32, (8, 128), 1)
    rows = []
    for l in range(4):
        halves = []
        for h in range(2):
            picked = jnp.zeros((8, 128), F32)
            for k in range(4):
                moved = pieces[h * 4 + k]
                if k != l:
                    moved = pltpu.roll(moved, ((k - l) * COL) % 128, 1)
                picked = jnp.where(lane // COL == k, moved, picked)
            halves.append(picked)
        rows.append(jnp.concatenate(halves, axis=0).astype(BF16))
    first = pltpu.roll(slab[8:16], lax.rem(128 - me * GB, 128), 1)
    second = pltpu.roll(slab[16:24], lax.rem(128 + 8 - me * GB, 128), 1)
    third = pltpu.roll(slab[8:16], 64 + 16 - me * GB, 1)
    rest = pltpu.roll(own_ref[...], 96, 1)
    extra = jnp.where(lane < 8, first, jnp.where(lane < 16, second, jnp.where(lane < 32, third, rest)))
    rows.append(jnp.concatenate([extra, jnp.zeros((8, 128), F32)], axis=0).astype(BF16))
    chunk = jnp.concatenate(rows, axis=0)

    def copy(n, carry):
        out_ref[n] = chunk
        return carry

    lax.fori_loop(0, NE, copy, 0, unroll=8)


def finish_kernel(got_ref, basis_ref, coef_ref, self_ref, rel_ref, own_ref):
    for h in range(2):
        for ib in range(32):
            n = h * 32 + ib
            for l in range(4):
                part = got_ref[n, l * 16 : l * 16 + 16, :].astype(F32)
                basis_ref[h * 4 + l, ib * 8 : ib * 8 + 8, 0:128] = part[0:8]
                basis_ref[h * 4 + l, ib * 8 : ib * 8 + 8, 128:256] = part[8:16]
            extra = got_ref[n, 64:80, :].astype(F32)[0:8]
            if n < 58:
                for t in range(3):
                    piece = extra if t == 0 else pltpu.roll(extra, 128 - 8 * t, 1)
                    rel_ref[n * REL_CHUNK + t * 8 : n * REL_CHUNK + t * 8 + 8, :] = piece
            if n < 32:
                own_ref[n * 8 : n * 8 + 8, :] = pltpu.roll(extra, 96, 1)
    for t in range(11):
        across = rel_ref[t * 128 : (t + 1) * 128, :].T[0:8, :]
        width = min(128, RELS - t * 128)
        coef_ref[:, t * 128 : t * 128 + width] = across[:, 0:width]
    self_ref[...] = own_ref[...].T[0:32, :]


def body(
    features,
    basis_stack,
    coeffs,
    self_weight,
    src_row,
    dst_row,
    rel_id,
    edge_weight,
    counts,
    out_grad,
):
    shape = jax.ShapeDtypeStruct
    me = lax.axis_index("rel").astype(jnp.int32).reshape(1)

    payload = call(
        share_kernel,
        shape((NK, W_ROWS, 256), BF16),
        [pltpu.VMEM((GB, REL_LANES), F32)],
    )(basis_stack, coeffs.T)
    weights = lax.all_to_all(payload, "rel", split_axis=0, concat_axis=0, tiled=True)

    def by_lane(a):
        return a.reshape(-1, NE, 4, 8).transpose(0, 2, 1, 3).reshape(-1, SLOTS)

    index = by_lane(jnp.stack([src_row, dst_row, rel_id]))
    live = jnp.arange(32, dtype=jnp.int32)[None, :] < counts[0][:, None]
    weight = by_lane(jnp.where(live, edge_weight, 0.0)[None])
    self_t = self_weight.T

    message, coef_slot = call(
        message_kernel,
        (shape((512, 128), BF16), shape((64, SLOTS), F32)),
        [pltpu.VMEM((64, REL_LANES), F32), pltpu.VMEM((SLOTS, 256), BF16), pltpu.VMEM((128, 512), F32)],
        flops=5_000_000_000,
    )(weights, features, index, weight)
    arrived = lax.all_to_all(message.reshape(NE, 8, 128), "ent", split_axis=0, concat_axis=0, tiled=True)

    back, layer_t, grad_t = call(
        node_kernel,
        (shape((512, 128), BF16), shape((COL, 256), BF16), shape((COL, 256), BF16)),
        [pltpu.VMEM((128, 512), F32)],
        flops=100_000_000,
    )(arrived.reshape(512, 128), index, features, self_t, out_grad.T)
    returned = lax.all_to_all(back.reshape(NE, 8, 128), "ent", split_axis=0, concat_axis=0, tiled=True)

    terms, input_t = call(
        grad_kernel,
        (shape((NE, G_ROWS, 128), BF16), shape((256, 256), BF16)),
        [
            pltpu.VMEM((SLOTS, 256), BF16),
            pltpu.VMEM((COL, SLOTS), F32),
            pltpu.VMEM((256, SLOTS), BF16),
            pltpu.VMEM((REL_PAD, SLOTS), BF16),
            pltpu.VMEM((SLOTS, SLOTS), BF16),
            pltpu.VMEM((64, SLOTS), F32),
        ],
        flops=8_000_000_000,
    )(returned.reshape(512, 128), weights, coef_slot, features, index, weight, self_t, grad_t)
    terms = lax.all_to_all(terms, "ent", split_axis=0, concat_axis=0, tiled=True)

    chunk, own = call(
        sum_kernel,
        (shape((NK, X_ROWS, 128), BF16), shape((8, 128), F32)),
    )(terms, input_t)
    chunk = lax.all_to_all(chunk, "rel", split_axis=0, concat_axis=0, tiled=True)

    merged, input_grad_t = call(
        merge_kernel,
        (shape((NE, G_ROWS, 128), BF16), shape((COL, 256), F32)),
        smem=1,
    )(me, chunk, own)
    gathered = lax.all_to_all(merged, "ent", split_axis=0, concat_axis=0, tiled=True)

    basis_grad, coef_t, self_grad_t = call(
        finish_kernel,
        (shape((GB, 256, 256), F32), shape((GB, RELS), F32), shape((COL, 256), F32)),
        [pltpu.VMEM((11 * 128, 128), F32), pltpu.VMEM((256, 128), F32)],
    )(gathered)
    return (layer_t.T, input_grad_t.T, coef_t.T, basis_grad, self_grad_t.T)


def solution(mesh):
    return jax.shard_map(
        body,
        mesh=mesh,
        in_specs=(
            P("ent", None),
            P("rel", None, None),
            P(None, "rel"),
            P(None, "rel"),
            P("ent", None),
            P("ent", None),
            P("ent", None),
            P("ent", None),
            P("ent", None),
            P("ent", "rel"),
        ),
        out_specs=(
            P("ent", "rel"),
            P("ent", "rel"),
            P(None, "rel"),
            P("rel", None, None),
            P(None, "rel"),
        ),
        check_vma=False,
    )
```

time: 772 us -> 185 us (0.24)
  waiting for transfers between devices: 434 us -> 24.1 us
  other arithmetic: 201 us -> 0.01 us
  blocking collectives: 12.7 us -> 122 us
  local copies, waits for them, and re-layouts: 44.1 us -> 2.64 us
  matrix products: 33.8 us -> 0 us
  Pallas kernels: 0 us -> 26.3 us
  starting transfers between devices: 29.6 us -> 7.84 us
  between operations: 14 us -> 0.78 us
    psum x2 -> x0, waiting for transfers between devices: 312 us -> none  [body(): lax.psum((coef_local, basis_local, self_local), 'ent')]
    scatter-add x3 -> x0, other arithmetic: 185 us -> none  [the longest x1 159 us: body(): jax.ops.segment_sum(scaled, src_flat, num_segments=row_count)]
    all_to_all x0 -> x4, blocking collectives: none -> 122 us  [the longest x1 41.7 us: body(): lax.all_to_all(merged, 'ent', split_axis=0, concat_axis=0, tiled=True)]
    reduce_scatter x2 -> x0, waiting for transfers between devices: 65.2 us -> none  [the longest x1 33.8 us: body(): lax.psum_scatter(input_local, 'rel', scatter_dimension=1, tiled=True)]
    dot_general x8 -> x0, matrix products: 33.8 us -> none  [the longest x1 17.9 us: body(): jnp.einsum('ebd,ed->eb', gathered, grad_msg, preferred_element_type=jnp.f...]
    all_to_all x2, waiting for transfers between devices: 56.6 us -> 24.1 us  [the longest x1 17.3 us: body(): lax.all_to_all(payload, 'rel', split_axis=0, concat_axis=0, tiled=True)]
    gather x3 -> x0, local copies, waits for them, and re-layouts: 30.8 us -> none  [the longest x1 15.7 us: body(): gathered = jnp.take(zvals, src_flat, axis=0)]
    pallas_call x0 -> x7, Pallas kernels: none -> 26.3 us  [run(): pl.pallas_call(kernel, out_shape=out_shape, in_specs=specs, out_specs=jax...]
  transfers between devices with their start and end apart: 6 -> 2, of which waited for: 6 -> 2; matrix products, arithmetic and copies ran while one was open for 1% -> 0% of each run, Pallas kernels for 0% -> 0%
where the time goes in v1:
time: 185 us; the launch traced here: 184 us
  blocking collectives  122 us (66%)
  Pallas kernels  26.3 us (14%)
  waiting for transfers between devices  24.1 us (13%)
  starting transfers between devices  7.84 us (4%)
  local copies, waits for them, and re-layouts  2.64 us (1%)
    all_to_all x1, blocking collectives, body(): lax.all_to_all(merged, 'ent', split_axis=0, concat_axis=0, tiled=True)  41.7 us
    all_to_all x1, blocking collectives, body(): lax.all_to_all(terms, 'ent', split_axis=0, concat_axis=0, tiled=True)  38.3 us
    pallas_call x7, Pallas kernels, run(): pl.pallas_call(kernel, out_shape=out_shape, in_specs=specs, out_specs=jax...  26.3 us
    all_to_all x1, blocking collectives, body(): lax.all_to_all(message.reshape(NE, 8, 128), 'ent', split_axis=0, concat_a...  25.6 us
    all_to_all x1, waiting for transfers between devices, body(): lax.all_to_all(payload, 'rel', split_axis=0, concat_axis=0, tiled=True)  17.3 us
    all_to_all x1, blocking collectives, body(): lax.all_to_all(back.reshape(NE, 8, 128), 'ent', split_axis=0, concat_axis...  16.7 us
    all_to_all x1, waiting for transfers between devices, body(): lax.all_to_all(chunk, 'rel', split_axis=0, concat_axis=0, tiled=True)  6.75 us
    all_to_all x1, starting transfers between devices, body(): lax.all_to_all(payload, 'rel', split_axis=0, concat_axis=0, tiled=True)  4.44 us
  transfers between devices with their start and end apart: 2, of which 2 were waited for; matrix products, arithmetic and copies ran while one was open for 0% of the time, Pallas kernels for 0%

profile of v1, /device:TPU:56, one launch (start us, length us, event | category | flops | bytes accessed | tf_op | source)
XLA Modules:
  0.0 183.9 jit_solution(17671239511425752564)
XLA Ops:
  0.6 1.2 copy-done
  1.9 0.8 copy-done.1
  2.6 1.4 shard_map.137
  4.0 0.0 copy-start.8
  4.1 4.4 %all-to-all-start = ((bf16[8,304,256]{2,1,0:T(8,128)(2,1)}), bf16[8,304,256]{2,1,0:T(8,128)(2,1)S(1)}, u32[]{:S(2)}, u32[]{:S(2)}) async-start(bf16[8,304,256]{2,1,0:T(8,128)(2,1)} %shard_map.137), calls=%async_computation | async-start | bytes 2490368 | tf_op jit(solution)/shard_map/all_to_all | solution.py:295
  8.5 0.1 copy.24
  8.6 0.1 reshape.40.weight_ref
  8.8 0.2 copy.23
  9.0 0.2 reshape.39.index_ref
  9.2 0.0 copy-start.3
  9.2 0.0 copy-start.4
  9.2 17.3 %all-to-all-done.w_ref = bf16[8,304,256]{2,1,0:T(8,128)(2,1)S(1)} async-done(((bf16[8,304,256]{2,1,0:T(8,128)(2,1)}), bf16[8,304,256]{2,1,0:T(8,128)(2,1)S(1)}, u32[]{:S(2)}, u32[]{:S(2)}) %all-to-all-start) | async-done | bytes 1245216 | tf_op jit(solution)/shard_map/all_to_all | solution.py:295
  26.6 5.2 %shard_map.138 = (bf16[512,128]{1,0:T(8,128)(2,1)S(1)}, f32[64,2048]{1,0:T(8,128)S(1)}) custom-call(bf16[8,304,256]{2,1,0:T(8,128)(2,1)S(1)} %all-to-all-done.w_ref, bf16[256,256]{1,0:T(8,128)(2,1)S(1)} %copy-done.2, s32[3,2048]{1,0:T(4,128)S(1)} %reshape.39.index_ref, f32[1,2048]{1,0:T(1,128)S(1)} %reshape.40.weight_ref), custom_call_target="tpu_custom_call" | custom-call | flops 5000000000 | bytes 4194304 | tf_op jit(solution)/shard_map/pallas_call | solution.py:51
  31.8 25.6 %all_to_all.30 = bf16[64,8,128]{2,1,0:T(8,128)(2,1)S(1)} all-to-all(bf16[64,8,128]{2,1,0:T(8,128)(2,1)S(1)} %bitcast.28), channel_id=1, replica_groups=mesh['ent'=64,'rel'=8] {'ent'}, dimensions={0} | all-to-all | bytes 262144 | tf_op jit(solution)/shard_map/all_to_all | solution.py:311
  57.4 1.4 shard_map.139
  58.7 16.7 %all_to_all.31 = bf16[64,8,128]{2,1,0:T(8,128)(2,1)S(1)} all-to-all(bf16[64,8,128]{2,1,0:T(8,128)(2,1)S(1)} %bitcast.27), channel_id=1, replica_groups=mesh['ent'=64,'rel'=8] {'ent'}, dimensions={0} | all-to-all | bytes 262144 | tf_op jit(solution)/shard_map/all_to_all | solution.py:319
  75.4 15.0 %shard_map.140 = (bf16[64,80,128]{2,1,0:T(8,128)(2,1)S(1)}, bf16[256,256]{1,0:T(8,128)(2,1)S(1)}) custom-call(bf16[512,128]{1,0:T(8,128)(2,1)S(1)} %bitcast.25, bf16[8,304,256]{2,1,0:T(8,128)(2,1)S(1)} %all-to-all-done.w_ref, f32[64,2048]{1,0:T(8,128)S(1)} %get-tuple-element.22.coef_ref, bf16[256,256]{1,0:T(8,128)(2,1)S(1)} %copy-done.2, ...), custom_call_target="tpu_custom_call" | custom-call | flops 8000000000 | bytes 4194304 | tf_op jit(solution)/shard_map/pallas_call | solution.py:51
  90.4 38.3 %all_to_all.32.got_ref = bf16[64,80,128]{2,1,0:T(8,128)(2,1)S(1)} all-to-all(bf16[64,80,128]{2,1,0:T(8,128)(2,1)S(1)} %get-tuple-element.24), channel_id=1, replica_groups=mesh['ent'=64,'rel'=8] {'ent'}, dimensions={0} | all-to-all | bytes 2621440 | tf_op jit(solution)/shard_map/all_to_all | solution.py:334
  128.7 0.9 shard_map.141
  129.6 3.4 %all-to-all-start.4 = ((bf16[8,96,128]{2,1,0:T(8,128)(2,1)}), bf16[8,96,128]{2,1,0:T(8,128)(2,1)S(1)}, u32[]{:S(2)}, u32[]{:S(2)}) async-start(bf16[8,96,128]{2,1,0:T(8,128)(2,1)} %get-tuple-element.26), calls=%async_computation.4 | async-start | bytes 393216 | tf_op jit(solution)/shard_map/all_to_all | solution.py:340
  133.0 6.8 %all-to-all-done.4.got_ref = bf16[8,96,128]{2,1,0:T(8,128)(2,1)S(1)} async-done(((bf16[8,96,128]{2,1,0:T(8,128)(2,1)}), bf16[8,96,128]{2,1,0:T(8,128)(2,1)S(1)}, u32[]{:S(2)}, u32[]{:S(2)}) %all-to-all-start.4) | async-done | bytes 196640 | tf_op jit(solution)/shard_map/all_to_all | solution.py:340
  139.7 0.8 shard_map.142
  140.5 41.7 %all_to_all.33.got_ref = bf16[64,80,128]{2,1,0:T(8,128)(2,1)S(1)} all-to-all(bf16[64,80,128]{2,1,0:T(8,128)(2,1)S(1)} %get-tuple-element.29), channel_id=1, replica_groups=mesh['ent'=64,'rel'=8] {'ent'}, dimensions={0} | all-to-all | bytes 2621440 | tf_op jit(solution)/shard_map/all_to_all | solution.py:347
  182.2 1.7 shard_map.143
  (17 shorter events, 0.0 us)
Async XLA Ops:
  0.6 1.2 copy-start
  1.9 0.8 copy-start.1
  4.0 4.5 %copy-start.5 = (f32[64,32]{0,1:T(8,128)S(1)}, f32[64,32]{0,1:T(8,128)}, u32[]{:S(2)}) copy-start(f32[64,32]{0,1:T(8,128)} %param.17) | copy-start | bytes 24580
  4.0 4.5 %copy-start.9 = (s32[1,64]{1,0:T(1,128)S(1)}, s32[1,64]{1,0:T(1,128)}, u32[]{:S(2)}) copy-start(s32[1,64]{1,0:T(1,128)} %param.18) | copy-start | bytes 772
  4.0 4.7 %copy-start.6 = (s32[64,32]{0,1:T(8,128)S(1)}, s32[64,32]{0,1:T(8,128)}, u32[]{:S(2)}) copy-start(s32[64,32]{0,1:T(8,128)} %param.16) | copy-start | bytes 24580
  4.0 4.7 %copy-start.7 = (s32[64,32]{0,1:T(8,128)S(1)}, s32[64,32]{0,1:T(8,128)}, u32[]{:S(2)}) copy-start(s32[64,32]{0,1:T(8,128)} %param.15) | copy-start | bytes 24580
  4.0 4.7 %copy-start.8 = (s32[64,32]{0,1:T(8,128)S(1)}, s32[64,32]{0,1:T(8,128)}, u32[]{:S(2)}) copy-start(s32[64,32]{0,1:T(8,128)} %param.14) | copy-start | bytes 24580
  4.0 22.5 %copy-start.2 = (bf16[256,256]{1,0:T(8,128)(2,1)S(1)}, bf16[256,256]{1,0:T(8,128)(2,1)}, u32[]{:S(2)}) copy-start(bf16[256,256]{1,0:T(8,128)(2,1)} %x_ref.5) | copy-start | bytes 393220
  4.1 22.5 %all-to-all-start = ((bf16[8,304,256]{2,1,0:T(8,128)(2,1)}), bf16[8,304,256]{2,1,0:T(8,128)(2,1)S(1)}, u32[]{:S(2)}, u32[]{:S(2)}) async-start(bf16[8,304,256]{2,1,0:T(8,128)(2,1)} %shard_map.137), calls=%async_computation | async-start | bytes 2490368 | tf_op jit(solution)/shard_map/all_to_all | solution.py:295
  9.2 48.2 %copy-start.3 = (bf16[256,32]{0,1:T(8,128)(2,1)S(1)}, bf16[256,32]{0,1:T(8,128)(2,1)}, u32[]{:S(2)}) copy-start(bf16[256,32]{0,1:T(8,128)(2,1)} %param.19) | copy-start | bytes 49156
  9.2 48.1 %copy-start.4 = (bf16[256,32]{0,1:T(8,128)(2,1)S(1)}, bf16[256,32]{0,1:T(8,128)(2,1)}, u32[]{:S(2)}) copy-start(bf16[256,32]{0,1:T(8,128)(2,1)} %param.13) | copy-start | bytes 49156
  129.6 10.2 %all-to-all-start.4 = ((bf16[8,96,128]{2,1,0:T(8,128)(2,1)}), bf16[8,96,128]{2,1,0:T(8,128)(2,1)S(1)}, u32[]{:S(2)}, u32[]{:S(2)}) async-start(bf16[8,96,128]{2,1,0:T(8,128)(2,1)} %get-tuple-element.26), calls=%async_computation.4 | async-start | bytes 393216 | tf_op jit(solution)/shard_map/all_to_all | solution.py:340

commit v2 on v1

v2 whole, which is shorter than its diff:
```python
import jax
import jax.numpy as jnp
from jax import lax
from jax.experimental import pallas as pl
from jax.experimental.pallas import tpu as pltpu
from jax.sharding import PartitionSpec as P


F32 = jnp.float32
BF16 = jnp.bfloat16

NE = 64
NK = 8
GB = 8
COL = 32
RELS = 1300
REL_CHUNK = 24
REL_PAD = 1344
REL_LANES = 1536
SLOTS = 2048
BLK = 256
W_ROWS = 304
G_TILES = 10
X_TILES = 11
F_TILES = 9


def nn(a, b):
    return lax.dot_general(a, b, (((1,), (0,)), ((), ())), preferred_element_type=F32)


def nt(a, b):
    return lax.dot_general(a, b, (((1,), (1,)), ((), ())), preferred_element_type=F32)


def tn(a, b):
    return lax.dot_general(a, b, (((0,), (0,)), ((), ())), preferred_element_type=F32)


def hot(rows, index):
    place = lax.broadcasted_iota(jnp.int32, (rows, index.shape[1]), 0)
    return jnp.where(place == index, 1.0, 0.0).astype(BF16)


def call(kernel, out_shape, scratch=(), flops=0, vmem=16, places="", out_places=""):
    space = {"s": pltpu.SMEM, "h": pltpu.HBM, "v": pltpu.VMEM}

    def spec(letters, n):
        return pl.BlockSpec(memory_space=space[letters[n] if n < len(letters) else "v"])

    def run(*args):
        outs = out_shape if isinstance(out_shape, tuple) else (out_shape,)
        results = pl.pallas_call(
            kernel,
            out_shape=outs,
            in_specs=[spec(places, n) for n in range(len(args))],
            out_specs=tuple(spec(out_places, n) for n in range(len(outs))),
            scratch_shapes=list(scratch),
            compiler_params=pltpu.CompilerParams(vmem_limit_bytes=vmem << 20),
            cost_estimate=pl.CostEstimate(flops=flops, bytes_accessed=4 << 20, transcendentals=0),
        )(*args)
        return results if len(outs) > 1 else results[0]

    return run


def share_kernel(basis_ref, coef_ref, out_ref, basis_buf, coef_buf, pad_ref, sems):
    copies = [pltpu.make_async_copy(basis_ref.at[l], basis_buf.at[l], sems.at[l]) for l in range(GB)]
    copies.append(pltpu.make_async_copy(coef_ref, coef_buf, sems.at[GB]))
    for copy in copies:
        copy.start()
    pad_ref[...] = jnp.zeros_like(pad_ref)
    for l in range(GB):
        copies[l].wait()
        turned = basis_buf[l].astype(F32).T.astype(BF16)
        for k in range(NK):
            out_ref[k, l * COL : (l + 1) * COL, :] = turned[k * COL : (k + 1) * COL, :]
    copies[GB].wait()
    pad_ref[:, 0:RELS] = coef_buf[...]
    for t in range(3):
        pair = jnp.concatenate(
            [pad_ref[:, t * 512 : t * 512 + 256], pad_ref[:, t * 512 + 256 : t * 512 + 512]], axis=0
        ).astype(BF16)
        for k in range(NK):
            out_ref[k, 256 + t * 16 : 256 + t * 16 + 16, :] = pair


def message_kernel(w_ref, x_ref, index_ref, weight_ref, out_ref, coef_ref, z_ref, coef_all, msg_ref):
    for g in range(NK):
        for t in range(3):
            pair = w_ref[g, 256 + t * 16 : 256 + t * 16 + 16, :].astype(F32)
            coef_all[g * GB : (g + 1) * GB, t * 512 : t * 512 + 256] = pair[0:8]
            coef_all[g * GB : (g + 1) * GB, t * 512 + 256 : t * 512 + 512] = pair[8:16]
        z_ref[g * 256 : (g + 1) * 256, :] = nt(w_ref[g, 0:256, :], x_ref[...]).astype(BF16)
    coef_table = coef_all[:, 0:REL_PAD].astype(BF16)
    for step in range(SLOTS // BLK):
        lanes = slice(step * BLK, (step + 1) * BLK)
        coef_ref[:, lanes] = nn(coef_table, hot(REL_PAD, index_ref[2:3, lanes]))
        source = hot(256, index_ref[0:1, lanes])
        total = jnp.zeros((COL, BLK), F32)
        for g in range(NK):
            taken = nn(z_ref[g * 256 : (g + 1) * 256, :], source)
            for l in range(GB):
                b = g * GB + l
                total += coef_ref[b : b + 1, lanes] * taken[l * COL : (l + 1) * COL, :]
        q, part = divmod(step * BLK, 512)
        msg_ref[q * COL : (q + 1) * COL, part : part + BLK] = total * weight_ref[0:1, lanes]
    out_ref[...] = msg_ref[...].T.astype(BF16)


def take_kernel(z_ref, index_ref, taken_ref, src_ref, rel_ref):
    def block(step, carry):
        lanes = pl.ds(pl.multiple_of(step * BLK, BLK), BLK)
        source = hot(256, index_ref[0:1, lanes])
        src_ref[:, lanes] = source
        rel_ref[:, lanes] = hot(REL_PAD, index_ref[2:3, lanes])
        for g in range(NK):
            rows = slice(g * 256, (g + 1) * 256)
            taken_ref[rows, lanes] = nn(z_ref[rows, :], source).astype(BF16)
        return carry

    lax.fori_loop(0, SLOTS // BLK, block, 0)


def node_kernel(got_ref, index_ref, x_ref, self_ref, out_grad_ref, out_ref, layer_ref, grad_ref, msg_ref):
    arrived = got_ref[...].astype(F32).T.astype(BF16)
    pre = nt(self_ref[...], x_ref[...])
    for q in range(4):
        lanes = slice(q * 512, (q + 1) * 512)
        pre += nt(arrived[q * COL : (q + 1) * COL, :], hot(256, index_ref[1:2, lanes]))
    sig = jax.nn.sigmoid(pre)
    layer_ref[...] = (pre * sig).astype(BF16)
    grad = (out_grad_ref[...].astype(F32) * sig * (1.0 + pre * (1.0 - sig))).astype(BF16)
    grad_ref[...] = grad
    for q in range(4):
        lanes = slice(q * 512, (q + 1) * 512)
        msg_ref[q * COL : (q + 1) * COL, :] = nn(grad, hot(256, index_ref[1:2, lanes]))
    out_ref[...] = msg_ref[...].T.astype(BF16)


def grad_kernel(
    taken_hbm,
    coef_hbm,
    src_hbm,
    rel_hbm,
    x_hbm,
    got_ref,
    weight_ref,
    grad_ref,
    grad_z_hbm,
    out_ref,
    taken_ref,
    coef_ref,
    src_ref,
    rel_ref,
    x_ref,
    grad_z_ref,
    m_ref,
    scaled_ref,
    part_ref,
    sems,
):
    pieces = [(coef_hbm, coef_ref)]
    for g in range(NK):
        rows = pl.ds(g * 256, 256)
        pieces.append((taken_hbm.at[rows], taken_ref.at[rows]))
    pieces += [(src_hbm, src_ref), (x_hbm, x_ref), (rel_hbm, rel_ref), (grad_z_ref, grad_z_hbm)]
    copies = [pltpu.make_async_copy(a, b, sems.at[n]) for n, (a, b) in enumerate(pieces)]
    for copy in copies[:12]:
        copy.start()
    arrived = got_ref[...].astype(F32).T
    for q in range(4):
        lanes = slice(q * 512, (q + 1) * 512)
        m_ref[:, lanes] = arrived[q * COL : (q + 1) * COL, :] * weight_ref[0:1, lanes]

    copies[0].wait()
    for half in range(2):
        for b in range(half * 32, half * 32 + 32, 2):
            if b % GB == 0:
                copies[1 + b // GB].wait()
            for step in range(SLOTS // BLK):
                lanes = slice(step * BLK, (step + 1) * BLK)
                m = m_ref[:, lanes]
                sums = []
                for one in (b, b + 1):
                    rows = slice(one * COL, (one + 1) * COL)
                    inner = taken_ref[rows, lanes].astype(F32) * m
                    sums.append((inner[0:8] + inner[8:16]) + (inner[16:24] + inner[24:32]))
                    scaled_ref[rows, lanes] = (coef_ref[one : one + 1, lanes] * m).astype(BF16)
                part_ref[b * 8 : b * 8 + 16, lanes] = jnp.concatenate(sums, axis=0).astype(BF16)
        if half == 0:
            copies[9].wait()
        rows = slice(half * 1024, (half + 1) * 1024)
        grad_z_ref[:, rows] = nt(src_ref[...], scaled_ref[rows, :]).astype(BF16)

    copies[12].start()
    copies[10].wait()
    turned = x_ref[...].astype(F32).T.astype(BF16)
    terms = nn(turned, grad_z_ref[...]).astype(BF16)
    for g in range(NK):
        for h in range(2):
            lanes = slice(g * 256 + h * 128, g * 256 + h * 128 + 128)
            out_ref[h * 32 : (h + 1) * 32, g] = terms[:, lanes].reshape(32, 8, 128)

    base = lax.broadcasted_iota(jnp.int32, (128, 512), 0) & 63
    fold = jnp.where(lax.broadcasted_iota(jnp.int32, (128, 512), 1) >> 3 == base, 1.0, 0.0).astype(BF16)
    copies[11].wait()
    coef = nt(rel_ref[...], nn(fold, part_ref[...]).astype(BF16))
    none = jnp.zeros((64, 256), BF16)
    own = nt(turned, jnp.concatenate([none, grad_ref[...], none[0:32]], axis=0))
    left = lax.broadcasted_iota(jnp.int32, (8, 128), 1) < 64
    empty = jnp.zeros((8, 128), F32)
    for n in range(NE):
        first = second = third = empty
        if (n + 1) * REL_CHUNK <= REL_PAD:
            first, second, third = (coef[n * REL_CHUNK + 8 * t : n * REL_CHUNK + 8 * t + 8] for t in range(3))
        rest = own[n * 8 : n * 8 + 8] if n < 32 else empty
        out_ref[n, 8] = jnp.where(left, first, third).astype(BF16)
        out_ref[n, 9] = jnp.where(left, second, rest).astype(BF16)
    copies[12].wait()


def input_kernel(grad_z_ref, w_ref, grad_ref, self_ref, input_ref):
    total = tn(grad_ref[...], self_ref[...])
    for g in range(NK):
        total += nn(grad_z_ref[:, g * 256 : (g + 1) * 256], w_ref[g, 0:256, :])
    input_ref[...] = total.T.astype(BF16)


def sum_kernel(got_ref, input_ref, out_ref, own_ref):
    def add(n, total):
        return total + got_ref[n].astype(F32)

    total = lax.fori_loop(0, NE, add, jnp.zeros((G_TILES, 8, 128), F32), unroll=8)
    own_ref[...] = total[9]
    slab = total[8:10].astype(BF16)
    for k in range(NK):
        for h in range(2):
            part = input_ref[k * COL : (k + 1) * COL, h * 128 : h * 128 + 128]
            out_ref[k, h * 4 : h * 4 + 4] = part.reshape(4, 8, 128)
        out_ref[k, 8] = total[k].astype(BF16)
        out_ref[k, 9:11] = slab


def merge_kernel(me_ref, got_ref, own_ref, out_ref, input_ref):
    me = me_ref[0]
    total = got_ref[0, 0:8].astype(F32)
    slab = got_ref[0, 9:11].astype(F32)
    pieces = [got_ref[0, 8].astype(F32)]
    for k in range(1, NK):
        total += got_ref[k, 0:8].astype(F32)
        slab += got_ref[k, 9:11].astype(F32)
        pieces.append(got_ref[k, 8].astype(F32))
    input_ref[:, 0:128] = total[0:4].reshape(32, 128)
    input_ref[:, 128:256] = total[4:8].reshape(32, 128)
    lane = lax.broadcasted_iota(jnp.int32, (8, 128), 1)
    tiles = []
    for l in range(4):
        for h in range(2):
            picked = jnp.zeros((8, 128), F32)
            for k in range(4):
                moved = pieces[h * 4 + k]
                if k != l:
                    moved = pltpu.roll(moved, ((k - l) * COL) % 128, 1)
                picked = jnp.where(lane >> 5 == k, moved, picked)
            tiles.append(picked)
    first = pltpu.roll(slab[0], lax.rem(128 - me * GB, 128), 1)
    second = pltpu.roll(slab[1], lax.rem(128 + 8 - me * GB, 128), 1)
    third = pltpu.roll(slab[0], 64 + 16 - me * GB, 1)
    rest = pltpu.roll(own_ref[...], 96, 1)
    tiles.append(jnp.where(lane < 8, first, jnp.where(lane < 16, second, jnp.where(lane < 32, third, rest))))
    chunk = jnp.stack(tiles).astype(BF16)

    def copy(n, carry):
        out_ref[n] = chunk
        return carry

    lax.fori_loop(0, NE, copy, 0, unroll=8)


def finish_kernel(got_ref, basis_ref, coef_ref, self_ref, rel_ref, own_ref):
    for n in range(NE):
        h, ib = divmod(n, 32)
        part = got_ref[n].astype(F32)
        for l in range(4):
            for o in range(2):
                basis_ref[h * 4 + l, ib * 8 : ib * 8 + 8, o * 128 : o * 128 + 128] = part[l * 2 + o]
        if n < 58:
            for t in range(3):
                piece = part[8] if t == 0 else pltpu.roll(part[8], 128 - 8 * t, 1)
                rel_ref[n * REL_CHUNK + t * 8 : n * REL_CHUNK + t * 8 + 8, :] = piece
        if n < 32:
            own_ref[n * 8 : n * 8 + 8, :] = pltpu.roll(part[8], 96, 1)
    for t in range(11):
        across = rel_ref[t * 128 : (t + 1) * 128, :].T[0:8, :]
        width = min(128, RELS - t * 128)
        coef_ref[:, t * 128 : t * 128 + width] = across[:, 0:width]
    self_ref[...] = own_ref[...].T[0:32, :]


def body(
    features,
    basis_stack,
    coeffs,
    self_weight,
    src_row,
    dst_row,
    rel_id,
    edge_weight,
    counts,
    out_grad,
):
    shape = jax.ShapeDtypeStruct
    me = lax.axis_index("rel").astype(jnp.int32).reshape(1)

    payload = call(
        share_kernel,
        shape((NK, W_ROWS, 256), BF16),
        [
            pltpu.VMEM((GB, 256, 256), BF16),
            pltpu.VMEM((GB, RELS), F32),
            pltpu.VMEM((GB, REL_LANES), F32),
            pltpu.SemaphoreType.DMA((GB + 1,)),
        ],
        places="hh",
    )(basis_stack, coeffs.T)
    weights = lax.all_to_all(payload, "rel", split_axis=0, concat_axis=0, tiled=True)

    def by_lane(a):
        return a.reshape(-1, NE, 4, 8).transpose(0, 2, 1, 3).reshape(-1, SLOTS)

    index = by_lane(jnp.stack([src_row, dst_row, rel_id]))
    live = jnp.arange(32, dtype=jnp.int32)[None, :] < counts[0][:, None]
    weight = by_lane(jnp.where(live, edge_weight, 0.0)[None])
    self_t = self_weight.T

    message, coef_slot, z = call(
        message_kernel,
        (shape((512, 128), BF16), shape((64, SLOTS), F32), shape((SLOTS, 256), BF16)),
        [pltpu.VMEM((64, REL_LANES), F32), pltpu.VMEM((128, 512), F32)],
        flops=5_000_000_000,
    )(weights, features, index, weight)
    arrived = lax.all_to_all(message.reshape(NE, 8, 128), "ent", split_axis=0, concat_axis=0, tiled=True)

    wide = shape((256, SLOTS), BF16)
    tall = shape((SLOTS, SLOTS), BF16)
    hots = shape((REL_PAD, SLOTS), BF16)
    taken, src_hot, rel_hot = call(take_kernel, (tall, wide, hots), flops=4_000_000_000, vmem=24)(z, index)
    back, layer_t, grad_t = call(
        node_kernel,
        (shape((512, 128), BF16), shape((COL, 256), BF16), shape((COL, 256), BF16)),
        [pltpu.VMEM((128, 512), F32)],
        flops=100_000_000,
    )(arrived.reshape(512, 128), index, features, self_t, out_grad.T)
    returned = lax.all_to_all(back.reshape(NE, 8, 128), "ent", split_axis=0, concat_axis=0, tiled=True)

    grad_z, terms = call(
        grad_kernel,
        (wide, shape((NE, G_TILES, 8, 128), BF16)),
        [
            pltpu.VMEM(tall.shape, BF16),
            pltpu.VMEM((64, SLOTS), F32),
            pltpu.VMEM(wide.shape, BF16),
            pltpu.VMEM(hots.shape, BF16),
            pltpu.VMEM((256, 256), BF16),
            pltpu.VMEM(wide.shape, BF16),
            pltpu.VMEM((COL, SLOTS), F32),
            pltpu.VMEM(tall.shape, BF16),
            pltpu.VMEM((512, SLOTS), BF16),
            pltpu.SemaphoreType.DMA((13,)),
        ],
        flops=8_000_000_000,
        vmem=40,
        places="hhhhh",
        out_places="h",
    )(taken, coef_slot, src_hot, rel_hot, features, returned.reshape(512, 128), weight, grad_t)
    terms = lax.all_to_all(terms, "ent", split_axis=0, concat_axis=0, tiled=True)
    input_t = call(input_kernel, shape((256, 256), BF16), flops=2_000_000_000)(grad_z, weights, grad_t, self_t)

    chunk, own = call(
        sum_kernel,
        (shape((NK, X_TILES, 8, 128), BF16), shape((8, 128), F32)),
    )(terms, input_t)
    chunk = lax.all_to_all(chunk, "rel", split_axis=0, concat_axis=0, tiled=True)

    merged, input_grad_t = call(
        merge_kernel,
        (shape((NE, F_TILES, 8, 128), BF16), shape((COL, 256), F32)),
        places="s",
    )(me, chunk, own)
    gathered = lax.all_to_all(merged, "ent", split_axis=0, concat_axis=0, tiled=True)

    basis_grad, coef_t, self_grad_t = call(
        finish_kernel,
        (shape((GB, 256, 256), F32), shape((GB, RELS), F32), shape((COL, 256), F32)),
        [pltpu.VMEM((11 * 128, 128), F32), pltpu.VMEM((256, 128), F32)],
    )(gathered)
    return (layer_t.T, input_grad_t.T, coef_t.T, basis_grad, self_grad_t.T)


def solution(mesh):
    return jax.shard_map(
        body,
        mesh=mesh,
        in_specs=(
            P("ent", None),
            P("rel", None, None),
            P(None, "rel"),
            P(None, "rel"),
            P("ent", None),
            P("ent", None),
            P("ent", None),
            P("ent", None),
            P("ent", None),
            P("ent", "rel"),
        ),
        out_specs=(
            P("ent", "rel"),
            P("ent", "rel"),
            P(None, "rel"),
            P("rel", None, None),
            P(None, "rel"),
        ),
        check_vma=False,
    )
```

time: 185 us -> 196 us (1.059)
  blocking collectives: 122 us -> 64.5 us
  waiting for transfers between devices: 24.1 us -> 54.5 us
  starting transfers between devices: 7.84 us -> 28 us
  local copies, waits for them, and re-layouts: 2.64 us -> 17.5 us
  Pallas kernels: 26.3 us -> 28.8 us
    all_to_all x2 -> x0, blocking collectives: 55 us -> none  [the longest x1 38.3 us: body(): lax.all_to_all(terms, 'ent', split_axis=0, concat_axis=0, tiled=True)]
    all_to_all x0 -> x2, waiting for transfers between devices: none -> 30.6 us  [the longest x1 30.6 us: body(): lax.all_to_all(terms, 'ent', split_axis=0, concat_axis=0, tiled=True)]
    all_to_all x0 -> x2, starting transfers between devices: none -> 20.2 us  [the longest x1 12.8 us: body(): lax.all_to_all(terms, 'ent', split_axis=0, concat_axis=0, tiled=True)]
    unnamed x20 -> x38, local copies, waits for them, and re-layouts: 2.05 us -> 16.9 us
    all_to_all x1, blocking collectives: 41.7 us -> 38.9 us  [body(): lax.all_to_all(merged, 'ent', split_axis=0, concat_axis=0, tiled=True)]
    pallas_call x7 -> x9, Pallas kernels: 26.3 us -> 28.8 us  [run(): pl.pallas_call(kernel, out_shape=outs, in_specs=[spec(places, n) for n in...]
  transfers between devices with their start and end apart: 2 -> 4, of which waited for: 2 -> 3; matrix products, arithmetic and copies ran while one was open for 0% -> 0% of each run, Pallas kernels for 0% -> 3%
where the time goes in v2:
time: 196 us; the launch traced here: 194 us
  blocking collectives  64.5 us (33%)
  waiting for transfers between devices  54.5 us (28%)
  Pallas kernels  28.8 us (15%)
  starting transfers between devices  28 us (14%)
  local copies, waits for them, and re-layouts  17.5 us (9%)
    all_to_all x1, blocking collectives, body(): lax.all_to_all(merged, 'ent', split_axis=0, concat_axis=0, tiled=True)  38.9 us
    all_to_all x1, waiting for transfers between devices, body(): lax.all_to_all(terms, 'ent', split_axis=0, concat_axis=0, tiled=True)  30.6 us
    pallas_call x9, Pallas kernels, run(): pl.pallas_call(kernel, out_shape=outs, in_specs=[spec(places, n) for n in...  28.8 us
    all_to_all x1, blocking collectives, body(): lax.all_to_all(message.reshape(NE, 8, 128), 'ent', split_axis=0, concat_a...  25.6 us
    all_to_all x1, waiting for transfers between devices, body(): lax.all_to_all(payload, 'rel', split_axis=0, concat_axis=0, tiled=True)  17.3 us
    unnamed x38, local copies, waits for them, and re-layouts  16.9 us
    all_to_all x1, starting transfers between devices, body(): lax.all_to_all(terms, 'ent', split_axis=0, concat_axis=0, tiled=True)  12.8 us
    all_to_all x1, starting transfers between devices, body(): lax.all_to_all(back.reshape(NE, 8, 128), 'ent', split_axis=0, concat_axis...  7.39 us
  transfers between devices with their start and end apart: 4, of which 3 were waited for; matrix products, arithmetic and copies ran while one was open for 0% of the time, Pallas kernels for 3%

profile of v2, /device:TPU:56, one launch (start us, length us, event | category | flops | bytes accessed | tf_op | source)
XLA Modules:
  0.0 194.3 jit_solution(8949623796914920984)
XLA Ops:
  0.6 1.2 copy-done
  2.6 3.4 %shard_map.137 = bf16[8,304,256]{2,1,0:T(8,128)(2,1)} custom-call(bf16[8,256,256]{2,1,0:T(8,128)(2,1)S(1)} %copy-done, f32[8,1300]{1,0:T(8,128)S(1)} %bitcast.28), custom_call_target="tpu_custom_call" | custom-call | bytes 4194304 | tf_op jit(solution)/shard_map/pallas_call | solution.py:53
  6.1 4.4 %all-to-all-start = ((bf16[8,304,256]{2,1,0:T(8,128)(2,1)}), bf16[8,304,256]{2,1,0:T(8,128)(2,1)S(1)}, u32[]{:S(2)}, u32[]{:S(2)}) async-start(bf16[8,304,256]{2,1,0:T(8,128)(2,1)} %shard_map.137), calls=%async_computation | async-start | bytes 2490368 | tf_op jit(solution)/shard_map/all_to_all | solution.py:327
  11.3 17.3 %all-to-all-done.w_ref = bf16[8,304,256]{2,1,0:T(8,128)(2,1)S(1)} async-done(((bf16[8,304,256]{2,1,0:T(8,128)(2,1)}), bf16[8,304,256]{2,1,0:T(8,128)(2,1)S(1)}, u32[]{:S(2)}, u32[]{:S(2)}) %all-to-all-start) | async-done | bytes 1245216 | tf_op jit(solution)/shard_map/all_to_all | solution.py:327
  28.6 4.1 %shard_map.138 = (bf16[512,128]{1,0:T(8,128)(2,1)S(1)}, f32[64,2048]{1,0:T(8,128)S(1)}, bf16[2048,256]{1,0:T(8,128)(2,1)S(1)}) custom-call(bf16[8,304,256]{2,1,0:T(8,128)(2,1)S(1)} %all-to-all-done.w_ref, bf16[256,256]{1,0:T(8,128)(2,1)S(1)} %copy-done.2, s32[3,2048]{1,0:T(4,128)S(1)} %reshape.39.index_ref, f32[1,2048]{1,0:T(1,128)S(1)} %reshape.40.weight_ref), custom_call_target="tpu_custom_call" | custom-call | flops 5000000000 | bytes 4194304 | tf_op jit(solution)/shard_map/pallas_call | solution.py:53
  33.7 25.6 %all_to_all.30 = bf16[64,8,128]{2,1,0:T(8,128)(2,1)S(1)} all-to-all(bf16[64,8,128]{2,1,0:T(8,128)(2,1)S(1)} %bitcast.27), channel_id=1, replica_groups=mesh['ent'=64,'rel'=8] {'ent'}, dimensions={0} | all-to-all | bytes 262144 | tf_op jit(solution)/shard_map/all_to_all | solution.py:343
  59.3 1.7 shard_map.139
  61.0 7.4 %all-to-all-start.2 = ((bf16[64,8,128]{2,1,0:T(8,128)(2,1)}), bf16[64,8,128]{2,1,0:T(8,128)(2,1)S(1)}, u32[]{:S(2)}, u32[]{:S(2)}) async-start(bf16[64,8,128]{2,1,0:T(8,128)(2,1)} %bitcast.14), calls=%async_computation.2 | async-start | bytes 262144 | tf_op jit(solution)/shard_map/all_to_all | solution.py:355
  68.4 1.2 copy-done.11
  69.6 5.8 %shard_map.140 = (bf16[2048,2048]{1,0:T(8,128)(2,1)S(1)}, bf16[256,2048]{1,0:T(8,128)(2,1)S(1)}, bf16[1344,2048]{1,0:T(8,128)(2,1)S(1)}) custom-call(bf16[2048,256]{1,0:T(8,128)(2,1)S(1)} %copy-done.11, s32[3,2048]{1,0:T(4,128)S(1)} %reshape.39.index_ref), custom_call_target="tpu_custom_call" | custom-call | flops 4000000000 | bytes 4194304 | tf_op jit(solution)/shard_map/pallas_call | solution.py:53
  75.4 3.3 %copy-done.5 = bf16[2048,2048]{1,0:T(8,128)(2,1)} copy-done((bf16[2048,2048]{1,0:T(8,128)(2,1)}, bf16[2048,2048]{1,0:T(8,128)(2,1)S(1)}, u32[]{:S(2)}) %copy-start.5) | copy-done | bytes 8388632
  78.7 2.5 %copy-done.8 = bf16[1344,2048]{1,0:T(8,128)(2,1)} copy-done((bf16[1344,2048]{1,0:T(8,128)(2,1)}, bf16[1344,2048]{1,0:T(8,128)(2,1)S(1)}, u32[]{:S(2)}) %copy-start.8) | copy-done | bytes 5505048
  81.2 1.0 copy-done.12
  82.1 2.6 %copy-done.9 = bf16[1344,2048]{1,0:T(8,128)(2,1)S(1)} copy-done((bf16[1344,2048]{1,0:T(8,128)(2,1)S(1)}, bf16[1344,2048]{1,0:T(8,128)(2,1)}, u32[]{:S(2)}) %copy-start.9) | copy-done | bytes 5505048
  84.7 1.2 copy-done.13
  85.9 10.0 %shard_map.141 = (bf16[256,2048]{1,0:T(8,128)(2,1)S(1)}, bf16[64,10,8,128]{3,2,1,0:T(8,128)(2,1)}) custom-call(bf16[2048,2048]{1,0:T(8,128)(2,1)} %copy-done.5, f32[64,2048]{1,0:T(8,128)S(1)} %get-tuple-element.27.coef_hbm, bf16[256,2048]{1,0:T(8,128)(2,1)S(1)} %copy-done.13, bf16[1344,2048]{1,0:T(8,128)(2,1)S(1)} %copy-done.9, ...), custom_call_target="tpu_custom_call" | custom-call | flops 8000000000 | bytes 4194304 | tf_op jit(solution)/shard_map/pallas_call | solution.py:53
  95.9 1.0 copy-done.6
  96.9 12.8 %all-to-all-start.3 = ((bf16[64,10,8,128]{3,2,1,0:T(8,128)(2,1)}), bf16[64,10,8,128]{3,2,1,0:T(8,128)(2,1)S(1)}, u32[]{:S(2)}, u32[]{:S(2)}) async-start(bf16[64,10,8,128]{3,2,1,0:T(8,128)(2,1)} %get-tuple-element.32), calls=%async_computation.3 | async-start | bytes 2621440 | tf_op jit(solution)/shard_map/all_to_all | solution.py:377
  109.7 1.2 copy-done.7
  111.4 30.6 %all-to-all-done.3.got_ref = bf16[64,10,8,128]{3,2,1,0:T(8,128)(2,1)S(1)} async-done(((bf16[64,10,8,128]{3,2,1,0:T(8,128)(2,1)}), bf16[64,10,8,128]{3,2,1,0:T(8,128)(2,1)S(1)}, u32[]{:S(2)}, u32[]{:S(2)}) %all-to-all-start.3) | async-done | bytes 1310752 | tf_op jit(solution)/shard_map/all_to_all | solution.py:377
  142.9 3.4 %all-to-all-start.4 = ((bf16[8,11,8,128]{3,2,1,0:T(8,128)(2,1)}), bf16[8,11,8,128]{3,2,1,0:T(8,128)(2,1)S(1)}, u32[]{:S(2)}, u32[]{:S(2)}) async-start(bf16[8,11,8,128]{3,2,1,0:T(8,128)(2,1)} %get-tuple-element.34), calls=%async_computation.4 | async-start | bytes 360448 | tf_op jit(solution)/shard_map/all_to_all | solution.py:384
  146.3 6.6 %all-to-all-done.4.got_ref = bf16[8,11,8,128]{3,2,1,0:T(8,128)(2,1)S(1)} async-done(((bf16[8,11,8,128]{3,2,1,0:T(8,128)(2,1)}), bf16[8,11,8,128]{3,2,1,0:T(8,128)(2,1)S(1)}, u32[]{:S(2)}, u32[]{:S(2)}) %all-to-all-start.4) | async-done | bytes 180256 | tf_op jit(solution)/shard_map/all_to_all | solution.py:384
  153.7 38.9 %all_to_all.31.got_ref = bf16[64,9,8,128]{3,2,1,0:T(8,128)(2,1)S(1)} all-to-all(bf16[64,9,8,128]{3,2,1,0:T(8,128)(2,1)S(1)} %get-tuple-element.37), channel_id=1, replica_groups=mesh['ent'=64,'rel'=8] {'ent'}, dimensions={0} | all-to-all | bytes 2359296 | tf_op jit(solution)/shard_map/all_to_all | solution.py:391
  192.7 1.6 shard_map.145
  (39 shorter events, 4.7 us)
Async XLA Ops:
  0.6 1.2 copy-start
  1.9 0.8 copy-start.1
  6.0 4.5 %copy-start.15 = (s32[64,32]{0,1:T(8,128)S(1)}, s32[64,32]{0,1:T(8,128)}, u32[]{:S(2)}) copy-start(s32[64,32]{0,1:T(8,128)} %param.16) | copy-start | bytes 24580
  6.0 4.5 %copy-start.16 = (s32[64,32]{0,1:T(8,128)S(1)}, s32[64,32]{0,1:T(8,128)}, u32[]{:S(2)}) copy-start(s32[64,32]{0,1:T(8,128)} %param.15) | copy-start | bytes 24580
  6.0 4.5 %copy-start.17 = (s32[64,32]{0,1:T(8,128)S(1)}, s32[64,32]{0,1:T(8,128)}, u32[]{:S(2)}) copy-start(s32[64,32]{0,1:T(8,128)} %param.14) | copy-start | bytes 24580
  6.0 4.9 %copy-start.14 = (f32[64,32]{0,1:T(8,128)S(1)}, f32[64,32]{0,1:T(8,128)}, u32[]{:S(2)}) copy-start(f32[64,32]{0,1:T(8,128)} %param.17) | copy-start | bytes 24580
  6.1 4.9 %copy-start.18 = (s32[1,64]{1,0:T(1,128)S(1)}, s32[1,64]{1,0:T(1,128)}, u32[]{:S(2)}) copy-start(s32[1,64]{1,0:T(1,128)} %param.18) | copy-start | bytes 772
  6.1 22.5 %copy-start.2 = (bf16[256,256]{1,0:T(8,128)(2,1)S(1)}, bf16[256,256]{1,0:T(8,128)(2,1)}, u32[]{:S(2)}) copy-start(bf16[256,256]{1,0:T(8,128)(2,1)} %x_hbm.1) | copy-start | bytes 393220
  6.1 22.5 %all-to-all-start = ((bf16[8,304,256]{2,1,0:T(8,128)(2,1)}), bf16[8,304,256]{2,1,0:T(8,128)(2,1)S(1)}, u32[]{:S(2)}, u32[]{:S(2)}) async-start(bf16[8,304,256]{2,1,0:T(8,128)(2,1)} %shard_map.137), calls=%async_computation | async-start | bytes 2490368 | tf_op jit(solution)/shard_map/all_to_all | solution.py:327
  11.2 48.1 %copy-start.3 = (bf16[256,32]{0,1:T(8,128)(2,1)S(1)}, bf16[256,32]{0,1:T(8,128)(2,1)}, u32[]{:S(2)}) copy-start(bf16[256,32]{0,1:T(8,128)(2,1)} %param.19) | copy-start | bytes 49156
  11.2 48.0 %copy-start.4 = (bf16[256,32]{0,1:T(8,128)(2,1)S(1)}, bf16[256,32]{0,1:T(8,128)(2,1)}, u32[]{:S(2)}) copy-start(bf16[256,32]{0,1:T(8,128)(2,1)} %param.13) | copy-start | bytes 49156
  32.7 1.0 copy-start.10
  61.0 21.2 %all-to-all-start.2 = ((bf16[64,8,128]{2,1,0:T(8,128)(2,1)}), bf16[64,8,128]{2,1,0:T(8,128)(2,1)S(1)}, u32[]{:S(2)}, u32[]{:S(2)}) async-start(bf16[64,8,128]{2,1,0:T(8,128)(2,1)} %bitcast.14), calls=%async_computation.2 | async-start | bytes 262144 | tf_op jit(solution)/shard_map/all_to_all | solution.py:355
  68.4 1.2 copy-start.11
  75.4 3.3 %copy-start.5 = (bf16[2048,2048]{1,0:T(8,128)(2,1)}, bf16[2048,2048]{1,0:T(8,128)(2,1)S(1)}, u32[]{:S(2)}) copy-start(bf16[2048,2048]{1,0:T(8,128)(2,1)S(1)} %get-tuple-element.26.taken_hbm) | copy-start | bytes 25165828
  78.7 2.5 %copy-start.8 = (bf16[1344,2048]{1,0:T(8,128)(2,1)}, bf16[1344,2048]{1,0:T(8,128)(2,1)S(1)}, u32[]{:S(2)}) copy-start(bf16[1344,2048]{1,0:T(8,128)(2,1)S(1)} %get-tuple-element.29.rel_hbm) | copy-start | bytes 16515076
  81.2 1.0 copy-start.12
  82.1 2.6 %copy-start.9 = (bf16[1344,2048]{1,0:T(8,128)(2,1)S(1)}, bf16[1344,2048]{1,0:T(8,128)(2,1)}, u32[]{:S(2)}) copy-start(bf16[1344,2048]{1,0:T(8,128)(2,1)} %copy-done.8) | copy-start | bytes 16515076
  84.7 1.2 copy-start.13
  95.9 1.0 copy-start.6
  96.9 45.2 %all-to-all-start.3 = ((bf16[64,10,8,128]{3,2,1,0:T(8,128)(2,1)}), bf16[64,10,8,128]{3,2,1,0:T(8,128)(2,1)S(1)}, u32[]{:S(2)}, u32[]{:S(2)}) async-start(bf16[64,10,8,128]{3,2,1,0:T(8,128)(2,1)} %get-tuple-element.32), calls=%async_computation.3 | async-start | bytes 2621440 | tf_op jit(solution)/shard_map/all_to_all | solution.py:377
  109.6 1.2 copy-start.7
  142.9 10.0 %all-to-all-start.4 = ((bf16[8,11,8,128]{3,2,1,0:T(8,128)(2,1)}), bf16[8,11,8,128]{3,2,1,0:T(8,128)(2,1)S(1)}, u32[]{:S(2)}, u32[]{:S(2)}) async-start(bf16[8,11,8,128]{3,2,1,0:T(8,128)(2,1)} %get-tuple-element.34), calls=%async_computation.4 | async-start | bytes 360448 | tf_op jit(solution)/shard_map/all_to_all | solution.py:384

commit v3 on v2

--- a/solution.py
+++ b/solution.py
@@ -42,7 +42,7 @@
     return jnp.where(place == index, 1.0, 0.0).astype(BF16)
 
 
-def call(kernel, out_shape, scratch=(), flops=0, vmem=16, places="", out_places=""):
+def call(kernel, out_shape, scratch=(), flops=0, vmem=60, places="", out_places=""):
     space = {"s": pltpu.SMEM, "h": pltpu.HBM, "v": pltpu.VMEM}
 
     def spec(letters, n):
@@ -85,6 +85,16 @@
             out_ref[k, 256 + t * 16 : 256 + t * 16 + 16, :] = pair
 
 
+def hot_kernel(index_ref, src_ref, rel_ref):
+    def block(step, carry):
+        lanes = pl.ds(pl.multiple_of(step * BLK, BLK), BLK)
+        src_ref[:, lanes] = hot(256, index_ref[0:1, lanes])
+        rel_ref[:, lanes] = hot(REL_PAD, index_ref[2:3, lanes])
+        return carry
+
+    lax.fori_loop(0, SLOTS // BLK, block, 0)
+
+
 def message_kernel(w_ref, x_ref, index_ref, weight_ref, out_ref, coef_ref, z_ref, coef_all, msg_ref):
     for g in range(NK):
         for t in range(3):
@@ -108,18 +118,21 @@
     out_ref[...] = msg_ref[...].T.astype(BF16)
 
 
-def take_kernel(z_ref, index_ref, taken_ref, src_ref, rel_ref):
-    def block(step, carry):
-        lanes = pl.ds(pl.multiple_of(step * BLK, BLK), BLK)
-        source = hot(256, index_ref[0:1, lanes])
-        src_ref[:, lanes] = source
-        rel_ref[:, lanes] = hot(REL_PAD, index_ref[2:3, lanes])
-        for g in range(NK):
-            rows = slice(g * 256, (g + 1) * 256)
+def take_kernel(w_ref, x_ref, index_ref, taken_hbm, z_ref, taken_ref, sems):
+    for g in range(NK):
+        z_ref[g * 256 : (g + 1) * 256, :] = nt(w_ref[g, 0:256, :], x_ref[...]).astype(BF16)
+    copies = []
+    for g in range(NK):
+        rows = slice(g * 256, (g + 1) * 256)
+        for step in range(SLOTS // BLK):
+            lanes = slice(step * BLK, (step + 1) * BLK)
+            source = hot(256, index_ref[0:1, lanes])
             taken_ref[rows, lanes] = nn(z_ref[rows, :], source).astype(BF16)
-        return carry
-
-    lax.fori_loop(0, SLOTS // BLK, block, 0)
+        place = pl.ds(g * 256, 256)
+        copies.append(pltpu.make_async_copy(taken_ref.at[place], taken_hbm.at[place], sems.at[g]))
+        copies[g].start()
+    for copy in copies:
+        copy.wait()
 
 
 def node_kernel(got_ref, index_ref, x_ref, self_ref, out_grad_ref, out_ref, layer_ref, grad_ref, msg_ref):
@@ -334,18 +347,25 @@
     weight = by_lane(jnp.where(live, edge_weight, 0.0)[None])
     self_t = self_weight.T
 
-    message, coef_slot, z = call(
+    wide = shape((256, SLOTS), BF16)
+    tall = shape((SLOTS, SLOTS), BF16)
+    hots = shape((REL_PAD, SLOTS), BF16)
+    src_hot, rel_hot = call(hot_kernel, (wide, hots), flops=4_000_000_000)(index)
+    message, coef_slot = call(
         message_kernel,
-        (shape((512, 128), BF16), shape((64, SLOTS), F32), shape((SLOTS, 256), BF16)),
-        [pltpu.VMEM((64, REL_LANES), F32), pltpu.VMEM((128, 512), F32)],
+        (shape((512, 128), BF16), shape((64, SLOTS), F32)),
+        [pltpu.VMEM((SLOTS, 256), BF16), pltpu.VMEM((64, REL_LANES), F32), pltpu.VMEM((128, 512), F32)],
         flops=5_000_000_000,
     )(weights, features, index, weight)
     arrived = lax.all_to_all(message.reshape(NE, 8, 128), "ent", split_axis=0, concat_axis=0, tiled=True)
 
-    wide = shape((256, SLOTS), BF16)
-    tall = shape((SLOTS, SLOTS), BF16)
-    hots = shape((REL_PAD, SLOTS), BF16)
-    taken, src_hot, rel_hot = call(take_kernel, (tall, wide, hots), flops=4_000_000_000, vmem=24)(z, index)
+    taken = call(
+        take_kernel,
+        tall,
+        [pltpu.VMEM((SLOTS, 256), BF16), pltpu.VMEM(tall.shape, BF16), pltpu.SemaphoreType.DMA((NK,))],
+        flops=4_000_000_000,
+        out_places="h",
+    )(weights, features, index)
     back, layer_t, grad_t = call(
         node_kernel,
         (shape((512, 128), BF16), shape((COL, 256), BF16), shape((COL, 256), BF16)),
@@ -370,7 +390,6 @@
             pltpu.SemaphoreType.DMA((13,)),
         ],
         flops=8_000_000_000,
-        vmem=40,
         places="hhhhh",
         out_places="h",
     )(taken, coef_slot, src_hot, rel_hot, features, returned.reshape(512, 128), weight, grad_t)

time: 196 us -> 194 us (0.990)
  blocking collectives: 64.5 us -> 39 us
  Pallas kernels: 28.8 us -> 43.9 us
  starting transfers between devices: 28 us -> 39.6 us
  local copies, waits for them, and re-layouts: 17.5 us -> 5.95 us
  waiting for transfers between devices: 54.5 us -> 62.5 us
    all_to_all x1 -> x0, blocking collectives: 25.6 us -> none  [body(): lax.all_to_all(message.reshape(NE, 8, 128), 'ent', split_axis=0, concat_a...]
    all_to_all x0 -> x1, starting transfers between devices: none -> 15.9 us  [body(): lax.all_to_all(message.reshape(NE, 8, 128), 'ent', split_axis=0, concat_a...]
    pallas_call x9 -> x10, Pallas kernels: 28.8 us -> 43.9 us  [run(): pl.pallas_call(kernel, out_shape=outs, in_specs=[spec(places, n) for n in...]
    unnamed x38 -> x20, local copies, waits for them, and re-layouts: 16.9 us -> 4.13 us
    all_to_all x0 -> x1, waiting for transfers between devices: none -> 5.21 us  [body(): lax.all_to_all(message.reshape(NE, 8, 128), 'ent', split_axis=0, concat_a...]
    all_to_all x1, starting transfers between devices: 12.8 us -> 8.34 us  [body(): lax.all_to_all(terms, 'ent', split_axis=0, concat_axis=0, tiled=True)]
    all_to_all x1, waiting for transfers between devices: 0.01 us -> 4.38 us  [body(): lax.all_to_all(back.reshape(NE, 8, 128), 'ent', split_axis=0, concat_axis...]
  transfers between devices with their start and end apart: 4 -> 5, of which waited for: 3 -> 5; matrix products, arithmetic and copies ran while one was open for 0% -> 1% of each run, Pallas kernels for 3% -> 7%
where the time goes in v3:
time: 194 us; the launch traced here: 192 us
  waiting for transfers between devices  62.5 us (32%)
  Pallas kernels  43.9 us (23%)
  starting transfers between devices  39.6 us (20%)
  blocking collectives  39 us (20%)
  local copies, waits for them, and re-layouts  5.95 us (3%)
    pallas_call x10, Pallas kernels, run(): pl.pallas_call(kernel, out_shape=outs, in_specs=[spec(places, n) for n in...  43.9 us
    all_to_all x1, blocking collectives, body(): lax.all_to_all(merged, 'ent', split_axis=0, concat_axis=0, tiled=True)  39 us
    all_to_all x1, waiting for transfers between devices, body(): lax.all_to_all(terms, 'ent', split_axis=0, concat_axis=0, tiled=True)  30.2 us
    all_to_all x1, waiting for transfers between devices, body(): lax.all_to_all(payload, 'rel', split_axis=0, concat_axis=0, tiled=True)  16.2 us
    all_to_all x1, starting transfers between devices, body(): lax.all_to_all(message.reshape(NE, 8, 128), 'ent', split_axis=0, concat_a...  15.9 us
    all_to_all x1, starting transfers between devices, body(): lax.all_to_all(terms, 'ent', split_axis=0, concat_axis=0, tiled=True)  8.34 us
    all_to_all x1, starting transfers between devices, body(): lax.all_to_all(back.reshape(NE, 8, 128), 'ent', split_axis=0, concat_axis...  7.5 us
    all_to_all x1, waiting for transfers between devices, body(): lax.all_to_all(chunk, 'rel', split_axis=0, concat_axis=0, tiled=True)  6.58 us
  transfers between devices with their start and end apart: 5, of which 5 were waited for; matrix products, arithmetic and copies ran while one was open for 1% of the time, Pallas kernels for 7%

profile of v3, /device:TPU:56, one launch (start us, length us, event | category | flops | bytes accessed | tf_op | source)
XLA Modules:
  0.0 191.7 jit_solution(924157865434568254)
XLA Ops:
  0.6 2.9 %shard_map.137 = bf16[8,304,256]{2,1,0:T(8,128)(2,1)} custom-call(bf16[8,256,256]{2,1,0:T(8,128)(2,1)} %basis_ref.1, f32[8,1300]{1,0:T(8,128)} %bitcast.30), custom_call_target="tpu_custom_call" | custom-call | bytes 4194304 | tf_op jit(solution)/shard_map/pallas_call | solution.py:53
  3.6 4.4 %all-to-all-start = ((bf16[8,304,256]{2,1,0:T(8,128)(2,1)}), bf16[8,304,256]{2,1,0:T(8,128)(2,1)S(1)}, u32[]{:S(2)}, u32[]{:S(2)}) async-start(bf16[8,304,256]{2,1,0:T(8,128)(2,1)} %shard_map.137), calls=%async_computation | async-start | bytes 2490368 | tf_op jit(solution)/shard_map/all_to_all | solution.py:340
  8.2 0.8 reshape.39.index_ref
  9.9 16.2 %all-to-all-done.w_ref = bf16[8,304,256]{2,1,0:T(8,128)(2,1)S(1)} async-done(((bf16[8,304,256]{2,1,0:T(8,128)(2,1)}), bf16[8,304,256]{2,1,0:T(8,128)(2,1)S(1)}, u32[]{:S(2)}, u32[]{:S(2)}) %all-to-all-start) | async-done | bytes 1245216 | tf_op jit(solution)/shard_map/all_to_all | solution.py:340
  26.1 1.0 copy-done.1
  27.1 6.0 %shard_map.138 = (bf16[512,128]{1,0:T(8,128)(2,1)}, f32[64,2048]{1,0:T(8,128)}) custom-call(bf16[8,304,256]{2,1,0:T(8,128)(2,1)} %copy-done.1, bf16[256,256]{1,0:T(8,128)(2,1)} %x_hbm.1, s32[3,2048]{1,0:T(4,128)} %reshape.39.index_ref, f32[1,2048]{1,0:T(1,128)} %reshape.40.weight_ref), custom_call_target="tpu_custom_call" | custom-call | flops 5000000000 | bytes 4194304 | tf_op jit(solution)/shard_map/pallas_call | solution.py:53
  33.2 15.9 %all-to-all-start.1 = ((bf16[64,8,128]{2,1,0:T(8,128)(2,1)}), bf16[64,8,128]{2,1,0:T(8,128)(2,1)S(1)}, u32[]{:S(2)}, u32[]{:S(2)}) async-start(bf16[64,8,128]{2,1,0:T(8,128)(2,1)} %bitcast.29), calls=%async_computation.1 | async-start | bytes 262144 | tf_op jit(solution)/shard_map/all_to_all | solution.py:360
  49.1 4.7 %shard_map.141 = (bf16[256,2048]{1,0:T(8,128)(2,1)}, bf16[1344,2048]{1,0:T(8,128)(2,1)}) custom-call(s32[3,2048]{1,0:T(4,128)} %reshape.39.index_ref), custom_call_target="tpu_custom_call" | custom-call | flops 4000000000 | bytes 4194304 | tf_op jit(solution)/shard_map/pallas_call | solution.py:53
  53.8 5.2 %all-to-all-done.1 = bf16[64,8,128]{2,1,0:T(8,128)(2,1)S(1)} async-done(((bf16[64,8,128]{2,1,0:T(8,128)(2,1)}), bf16[64,8,128]{2,1,0:T(8,128)(2,1)S(1)}, u32[]{:S(2)}, u32[]{:S(2)}) %all-to-all-start.1) | async-done | bytes 131104 | tf_op jit(solution)/shard_map/all_to_all | solution.py:360
  59.6 2.7 %shard_map.139 = (bf16[512,128]{1,0:T(8,128)(2,1)}, bf16[32,256]{1,0:T(8,128)(2,1)}, bf16[32,256]{1,0:T(8,128)(2,1)}) custom-call(bf16[512,128]{1,0:T(8,128)(2,1)} %bitcast.27, s32[3,2048]{1,0:T(4,128)} %reshape.39.index_ref, bf16[256,256]{1,0:T(8,128)(2,1)} %x_hbm.1, bf16[32,256]{1,0:T(8,128)(2,1)} %bitcast.39, bf16[32,256]{1,0:T(8,128)(2,1)} %bitcast.38), custom_call_target="tpu_custom_call" | custom-call | flops 100000000 | bytes 4194304 | tf_op jit(solution)/shard_map/pallas_call | solution.py:53
  62.3 7.5 %all-to-all-start.2 = ((bf16[64,8,128]{2,1,0:T(8,128)(2,1)}), bf16[64,8,128]{2,1,0:T(8,128)(2,1)S(1)}, u32[]{:S(2)}, u32[]{:S(2)}) async-start(bf16[64,8,128]{2,1,0:T(8,128)(2,1)} %bitcast.28), calls=%async_computation.2 | async-start | bytes 262144 | tf_op jit(solution)/shard_map/all_to_all | solution.py:375
  69.8 5.5 %shard_map.140.taken_hbm = bf16[2048,2048]{1,0:T(8,128)(2,1)} custom-call(bf16[8,304,256]{2,1,0:T(8,128)(2,1)} %copy-done.1, bf16[256,256]{1,0:T(8,128)(2,1)} %x_hbm.1, s32[3,2048]{1,0:T(4,128)} %reshape.39.index_ref), custom_call_target="tpu_custom_call" | custom-call | flops 4000000000 | bytes 4194304 | tf_op jit(solution)/shard_map/pallas_call | solution.py:53
  75.4 4.4 %all-to-all-done.2 = bf16[64,8,128]{2,1,0:T(8,128)(2,1)S(1)} async-done(((bf16[64,8,128]{2,1,0:T(8,128)(2,1)}), bf16[64,8,128]{2,1,0:T(8,128)(2,1)S(1)}, u32[]{:S(2)}, u32[]{:S(2)}) %all-to-all-start.2) | async-done | bytes 131104 | tf_op jit(solution)/shard_map/all_to_all | solution.py:375
  80.4 11.9 %shard_map.142 = (bf16[256,2048]{1,0:T(8,128)(2,1)}, bf16[64,10,8,128]{3,2,1,0:T(8,128)(2,1)}) custom-call(bf16[2048,2048]{1,0:T(8,128)(2,1)} %shard_map.140.taken_hbm, f32[64,2048]{1,0:T(8,128)} %get-tuple-element.23.coef_hbm, bf16[256,2048]{1,0:T(8,128)(2,1)} %get-tuple-element.24.src_hbm, bf16[1344,2048]{1,0:T(8,128)(2,1)} %get-tuple-element.25.rel_hbm, ...), custom_call_target="tpu_custom_call" | custom-call | flops 8000000000 | bytes 4194304 | tf_op jit(solution)/shard_map/pallas_call | solution.py:53
  92.3 8.3 %all-to-all-start.3 = ((bf16[64,10,8,128]{3,2,1,0:T(8,128)(2,1)}), bf16[64,10,8,128]{3,2,1,0:T(8,128)(2,1)S(1)}, u32[]{:S(2)}, u32[]{:S(2)}) async-start(bf16[64,10,8,128]{3,2,1,0:T(8,128)(2,1)} %get-tuple-element.28), calls=%async_computation.3 | async-start | bytes 2621440 | tf_op jit(solution)/shard_map/all_to_all | solution.py:396
  100.7 2.8 %shard_map.143.input_ref = bf16[256,256]{1,0:T(8,128)(2,1)} custom-call(bf16[256,2048]{1,0:T(8,128)(2,1)} %get-tuple-element.29.grad_z_ref, bf16[8,304,256]{2,1,0:T(8,128)(2,1)} %copy-done.1, bf16[32,256]{1,0:T(8,128)(2,1)} %get-tuple-element.27.grad_ref, bf16[32,256]{1,0:T(8,128)(2,1)} %bitcast.40), custom_call_target="tpu_custom_call" | custom-call | flops 2000000000 | bytes 4194304 | tf_op jit(solution)/shard_map/pallas_call | solution.py:53
  103.5 30.2 %all-to-all-done.3.got_ref = bf16[64,10,8,128]{3,2,1,0:T(8,128)(2,1)S(1)} async-done(((bf16[64,10,8,128]{3,2,1,0:T(8,128)(2,1)}), bf16[64,10,8,128]{3,2,1,0:T(8,128)(2,1)S(1)}, u32[]{:S(2)}, u32[]{:S(2)}) %all-to-all-start.3) | async-done | bytes 1310752 | tf_op jit(solution)/shard_map/all_to_all | solution.py:396
  133.7 1.1 copy-done
  134.7 2.2 %shard_map.144 = (bf16[8,11,8,128]{3,2,1,0:T(8,128)(2,1)}, f32[8,128]{1,0:T(8,128)}) custom-call(bf16[64,10,8,128]{3,2,1,0:T(8,128)(2,1)} %copy-done, bf16[256,256]{1,0:T(8,128)(2,1)} %shard_map.143.input_ref), custom_call_target="tpu_custom_call" | custom-call | bytes 4194304 | tf_op jit(solution)/shard_map/pallas_call | solution.py:53
  137.0 3.4 %all-to-all-start.4 = ((bf16[8,11,8,128]{3,2,1,0:T(8,128)(2,1)}), bf16[8,11,8,128]{3,2,1,0:T(8,128)(2,1)S(1)}, u32[]{:S(2)}, u32[]{:S(2)}) async-start(bf16[8,11,8,128]{3,2,1,0:T(8,128)(2,1)} %get-tuple-element.30), calls=%async_computation.4 | async-start | bytes 360448 | tf_op jit(solution)/shard_map/all_to_all | solution.py:403
  140.4 6.6 %all-to-all-done.4.got_ref = bf16[8,11,8,128]{3,2,1,0:T(8,128)(2,1)S(1)} async-done(((bf16[8,11,8,128]{3,2,1,0:T(8,128)(2,1)}), bf16[8,11,8,128]{3,2,1,0:T(8,128)(2,1)S(1)}, u32[]{:S(2)}, u32[]{:S(2)}) %all-to-all-start.4) | async-done | bytes 180256 | tf_op jit(solution)/shard_map/all_to_all | solution.py:403
  147.6 2.1 %shard_map.145 = (bf16[64,9,8,128]{3,2,1,0:T(8,128)(2,1)}, f32[32,256]{1,0:T(8,128)}) custom-call(s32[1]{0:T(128)} %bitcast.13.me_ref, bf16[8,11,8,128]{3,2,1,0:T(8,128)(2,1)} %copy-done.2, f32[8,128]{1,0:T(8,128)} %get-tuple-element.31.own_ref), custom_call_target="tpu_custom_call" | custom-call | bytes 4194304 | tf_op jit(solution)/shard_map/pallas_call | solution.py:53
  149.7 39.0 %all_to_all.30.got_ref = bf16[64,9,8,128]{3,2,1,0:T(8,128)(2,1)} all-to-all(bf16[64,9,8,128]{3,2,1,0:T(8,128)(2,1)} %get-tuple-element.33), channel_id=1, replica_groups=mesh['ent'=64,'rel'=8] {'ent'}, dimensions={0} | all-to-all | bytes 2359296 | tf_op jit(solution)/shard_map/all_to_all | solution.py:410
  188.7 3.0 %shard_map.146 = (f32[8,256,256]{2,1,0:T(8,128)}, f32[8,1300]{1,0:T(8,128)}, f32[32,256]{1,0:T(8,128)}) custom-call(bf16[64,9,8,128]{3,2,1,0:T(8,128)(2,1)} %all_to_all.30.got_ref), custom_call_target="tpu_custom_call" | custom-call | bytes 4194304 | tf_op jit(solution)/shard_map/pallas_call | solution.py:53
  (23 shorter events, 3.0 us)
Async XLA Ops:
  3.5 4.5 %copy-start.6 = (s32[64,32]{0,1:T(8,128)S(1)}, s32[64,32]{0,1:T(8,128)}, u32[]{:S(2)}) copy-start(s32[64,32]{0,1:T(8,128)} %param.16) | copy-start | bytes 24580
  3.5 4.5 %copy-start.7 = (s32[64,32]{0,1:T(8,128)S(1)}, s32[64,32]{0,1:T(8,128)}, u32[]{:S(2)}) copy-start(s32[64,32]{0,1:T(8,128)} %param.15) | copy-start | bytes 24580
  3.5 4.5 %copy-start.8 = (s32[64,32]{0,1:T(8,128)S(1)}, s32[64,32]{0,1:T(8,128)}, u32[]{:S(2)}) copy-start(s32[64,32]{0,1:T(8,128)} %param.14) | copy-start | bytes 24580
  3.6 5.5 %copy-start.5 = (f32[64,32]{0,1:T(8,128)S(1)}, f32[64,32]{0,1:T(8,128)}, u32[]{:S(2)}) copy-start(f32[64,32]{0,1:T(8,128)} %param.17) | copy-start | bytes 24580
  3.6 5.5 %copy-start.9 = (s32[1,64]{1,0:T(1,128)S(1)}, s32[1,64]{1,0:T(1,128)}, u32[]{:S(2)}) copy-start(s32[1,64]{1,0:T(1,128)} %param.18) | copy-start | bytes 772
  3.6 22.5 %all-to-all-start = ((bf16[8,304,256]{2,1,0:T(8,128)(2,1)}), bf16[8,304,256]{2,1,0:T(8,128)(2,1)S(1)}, u32[]{:S(2)}, u32[]{:S(2)}) async-start(bf16[8,304,256]{2,1,0:T(8,128)(2,1)} %shard_map.137), calls=%async_computation | async-start | bytes 2490368 | tf_op jit(solution)/shard_map/all_to_all | solution.py:340
  26.1 1.0 copy-start.1
  33.2 25.8 %all-to-all-start.1 = ((bf16[64,8,128]{2,1,0:T(8,128)(2,1)}), bf16[64,8,128]{2,1,0:T(8,128)(2,1)S(1)}, u32[]{:S(2)}, u32[]{:S(2)}) async-start(bf16[64,8,128]{2,1,0:T(8,128)(2,1)} %bitcast.29), calls=%async_computation.1 | async-start | bytes 262144 | tf_op jit(solution)/shard_map/all_to_all | solution.py:360
  59.0 0.7 copy-start.4
  62.3 17.4 %all-to-all-start.2 = ((bf16[64,8,128]{2,1,0:T(8,128)(2,1)}), bf16[64,8,128]{2,1,0:T(8,128)(2,1)S(1)}, u32[]{:S(2)}, u32[]{:S(2)}) async-start(bf16[64,8,128]{2,1,0:T(8,128)(2,1)} %bitcast.28), calls=%async_computation.2 | async-start | bytes 262144 | tf_op jit(solution)/shard_map/all_to_all | solution.py:375
  79.8 0.7 copy-start.3
  92.3 41.4 %all-to-all-start.3 = ((bf16[64,10,8,128]{3,2,1,0:T(8,128)(2,1)}), bf16[64,10,8,128]{3,2,1,0:T(8,128)(2,1)S(1)}, u32[]{:S(2)}, u32[]{:S(2)}) async-start(bf16[64,10,8,128]{3,2,1,0:T(8,128)(2,1)} %get-tuple-element.28), calls=%async_computation.3 | async-start | bytes 2621440 | tf_op jit(solution)/shard_map/all_to_all | solution.py:396
  133.7 1.1 copy-start
  137.0 10.0 %all-to-all-start.4 = ((bf16[8,11,8,128]{3,2,1,0:T(8,128)(2,1)}), bf16[8,11,8,128]{3,2,1,0:T(8,128)(2,1)S(1)}, u32[]{:S(2)}, u32[]{:S(2)}) async-start(bf16[8,11,8,128]{3,2,1,0:T(8,128)(2,1)} %get-tuple-element.30), calls=%async_computation.4 | async-start | bytes 360448 | tf_op jit(solution)/shard_map/all_to_all | solution.py:403
  146.9 0.7 copy-start.2

commit v4 on v2

--- a/solution.py
+++ b/solution.py
@@ -64,18 +64,17 @@
     return run
 
 
-def share_kernel(basis_ref, coef_ref, out_ref, basis_buf, coef_buf, pad_ref, sems):
-    copies = [pltpu.make_async_copy(basis_ref.at[l], basis_buf.at[l], sems.at[l]) for l in range(GB)]
-    copies.append(pltpu.make_async_copy(coef_ref, coef_buf, sems.at[GB]))
-    for copy in copies:
-        copy.start()
+def share_kernel(basis_ref, coef_ref, out_hbm, basis_buf, coef_buf, pad_ref, out_ref, sems, out_sems):
+    loads = [pltpu.make_async_copy(coef_ref, coef_buf, sems.at[GB])]
+    loads += [pltpu.make_async_copy(basis_ref.at[l], basis_buf.at[l], sems.at[l]) for l in range(GB)]
+    for load in loads:
+        load.start()
+    stores = []
+    for n in range(GB + 1):
+        rows = pl.ds(256, W_ROWS - 256) if n == 0 else pl.ds((n - 1) * COL, COL)
+        stores.append(pltpu.make_async_copy(out_ref.at[:, rows], out_hbm.at[:, rows], out_sems.at[n]))
     pad_ref[...] = jnp.zeros_like(pad_ref)
-    for l in range(GB):
-        copies[l].wait()
-        turned = basis_buf[l].astype(F32).T.astype(BF16)
-        for k in range(NK):
-            out_ref[k, l * COL : (l + 1) * COL, :] = turned[k * COL : (k + 1) * COL, :]
-    copies[GB].wait()
+    loads[0].wait()
     pad_ref[:, 0:RELS] = coef_buf[...]
     for t in range(3):
         pair = jnp.concatenate(
@@ -83,6 +82,15 @@
         ).astype(BF16)
         for k in range(NK):
             out_ref[k, 256 + t * 16 : 256 + t * 16 + 16, :] = pair
+    stores[0].start()
+    for l in range(GB):
+        loads[l + 1].wait()
+        turned = basis_buf[l].astype(F32).T.astype(BF16)
+        for k in range(NK):
+            out_ref[k, l * COL : (l + 1) * COL, :] = turned[k * COL : (k + 1) * COL, :]
+        stores[l + 1].start()
+    for store in stores:
+        store.wait()
 
 
 def message_kernel(w_ref, x_ref, index_ref, weight_ref, out_ref, coef_ref, z_ref, coef_all, msg_ref):
@@ -108,20 +116,6 @@
     out_ref[...] = msg_ref[...].T.astype(BF16)
 
 
-def take_kernel(z_ref, index_ref, taken_ref, src_ref, rel_ref):
-    def block(step, carry):
-        lanes = pl.ds(pl.multiple_of(step * BLK, BLK), BLK)
-        source = hot(256, index_ref[0:1, lanes])
-        src_ref[:, lanes] = source
-        rel_ref[:, lanes] = hot(REL_PAD, index_ref[2:3, lanes])
-        for g in range(NK):
-            rows = slice(g * 256, (g + 1) * 256)
-            taken_ref[rows, lanes] = nn(z_ref[rows, :], source).astype(BF16)
-        return carry
-
-    lax.fori_loop(0, SLOTS // BLK, block, 0)
-
-
 def node_kernel(got_ref, index_ref, x_ref, self_ref, out_grad_ref, out_ref, layer_ref, grad_ref, msg_ref):
     arrived = got_ref[...].astype(F32).T.astype(BF16)
     pre = nt(self_ref[...], x_ref[...])
@@ -139,62 +133,55 @@
 
 
 def grad_kernel(
-    taken_hbm,
-    coef_hbm,
-    src_hbm,
-    rel_hbm,
-    x_hbm,
     got_ref,
+    w_ref,
+    coef_ref,
+    x_ref,
+    index_ref,
     weight_ref,
+    self_ref,
     grad_ref,
-    grad_z_hbm,
     out_ref,
-    taken_ref,
-    coef_ref,
+    input_ref,
+    w_all,
+    z_ref,
     src_ref,
     rel_ref,
-    x_ref,
     grad_z_ref,
     m_ref,
     scaled_ref,
     part_ref,
-    sems,
 ):
-    pieces = [(coef_hbm, coef_ref)]
-    for g in range(NK):
-        rows = pl.ds(g * 256, 256)
-        pieces.append((taken_hbm.at[rows], taken_ref.at[rows]))
-    pieces += [(src_hbm, src_ref), (x_hbm, x_ref), (rel_hbm, rel_ref), (grad_z_ref, grad_z_hbm)]
-    copies = [pltpu.make_async_copy(a, b, sems.at[n]) for n, (a, b) in enumerate(pieces)]
-    for copy in copies[:12]:
-        copy.start()
     arrived = got_ref[...].astype(F32).T
     for q in range(4):
         lanes = slice(q * 512, (q + 1) * 512)
         m_ref[:, lanes] = arrived[q * COL : (q + 1) * COL, :] * weight_ref[0:1, lanes]
-
-    copies[0].wait()
+    for g in range(NK):
+        w_all[g * 256 : (g + 1) * 256, :] = w_ref[g, 0:256, :]
+    z_ref[...] = nt(w_all[...], x_ref[...]).astype(BF16)
+
+    for step in range(SLOTS // BLK):
+        lanes = slice(step * BLK, (step + 1) * BLK)
+        source = hot(256, index_ref[0:1, lanes])
+        src_ref[:, lanes] = source
+        rel_ref[:, lanes] = hot(REL_PAD, index_ref[2:3, lanes])
+        m = m_ref[:, lanes]
+        for g in range(NK):
+            taken = nn(z_ref[g * 256 : (g + 1) * 256, :], source)
+            for l in range(0, GB, 2):
+                sums = []
+                for one in (l, l + 1):
+                    b = g * GB + one
+                    inner = taken[one * COL : (one + 1) * COL, :] * m
+                    sums.append((inner[0:8] + inner[8:16]) + (inner[16:24] + inner[24:32]))
+                    scaled_ref[b * COL : (b + 1) * COL, lanes] = (coef_ref[b : b + 1, lanes] * m).astype(BF16)
+                rows = slice((g * GB + l) * 8, (g * GB + l) * 8 + 16)
+                part_ref[rows, lanes] = jnp.concatenate(sums, axis=0).astype(BF16)
+
     for half in range(2):
-        for b in range(half * 32, half * 32 + 32, 2):
-            if b % GB == 0:
-                copies[1 + b // GB].wait()
-            for step in range(SLOTS // BLK):
-                lanes = slice(step * BLK, (step + 1) * BLK)
-                m = m_ref[:, lanes]
-                sums = []
-                for one in (b, b + 1):
-                    rows = slice(one * COL, (one + 1) * COL)
-                    inner = taken_ref[rows, lanes].astype(F32) * m
-                    sums.append((inner[0:8] + inner[8:16]) + (inner[16:24] + inner[24:32]))
-                    scaled_ref[rows, lanes] = (coef_ref[one : one + 1, lanes] * m).astype(BF16)
-                part_ref[b * 8 : b * 8 + 16, lanes] = jnp.concatenate(sums, axis=0).astype(BF16)
-        if half == 0:
-            copies[9].wait()
         rows = slice(half * 1024, (half + 1) * 1024)
         grad_z_ref[:, rows] = nt(src_ref[...], scaled_ref[rows, :]).astype(BF16)
 
-    copies[12].start()
-    copies[10].wait()
     turned = x_ref[...].astype(F32).T.astype(BF16)
     terms = nn(turned, grad_z_ref[...]).astype(BF16)
     for g in range(NK):
@@ -204,7 +191,6 @@
 
     base = lax.broadcasted_iota(jnp.int32, (128, 512), 0) & 63
     fold = jnp.where(lax.broadcasted_iota(jnp.int32, (128, 512), 1) >> 3 == base, 1.0, 0.0).astype(BF16)
-    copies[11].wait()
     coef = nt(rel_ref[...], nn(fold, part_ref[...]).astype(BF16))
     none = jnp.zeros((64, 256), BF16)
     own = nt(turned, jnp.concatenate([none, grad_ref[...], none[0:32]], axis=0))
@@ -217,13 +203,7 @@
         rest = own[n * 8 : n * 8 + 8] if n < 32 else empty
         out_ref[n, 8] = jnp.where(left, first, third).astype(BF16)
         out_ref[n, 9] = jnp.where(left, second, rest).astype(BF16)
-    copies[12].wait()
-
-
-def input_kernel(grad_z_ref, w_ref, grad_ref, self_ref, input_ref):
-    total = tn(grad_ref[...], self_ref[...])
-    for g in range(NK):
-        total += nn(grad_z_ref[:, g * 256 : (g + 1) * 256], w_ref[g, 0:256, :])
+    total = tn(grad_ref[...], self_ref[...]) + nn(grad_z_ref[...], w_all[...])
     input_ref[...] = total.T.astype(BF16)
 
 
@@ -320,9 +300,13 @@
             pltpu.VMEM((GB, 256, 256), BF16),
             pltpu.VMEM((GB, RELS), F32),
             pltpu.VMEM((GB, REL_LANES), F32),
+            pltpu.VMEM((NK, W_ROWS, 256), BF16),
+            pltpu.SemaphoreType.DMA((GB + 1,)),
             pltpu.SemaphoreType.DMA((GB + 1,)),
         ],
+        vmem=60,
         places="hh",
+        out_places="h",
     )(basis_stack, coeffs.T)
     weights = lax.all_to_all(payload, "rel", split_axis=0, concat_axis=0, tiled=True)
 
@@ -334,18 +318,14 @@
     weight = by_lane(jnp.where(live, edge_weight, 0.0)[None])
     self_t = self_weight.T
 
-    message, coef_slot, z = call(
+    message, coef_slot = call(
         message_kernel,
-        (shape((512, 128), BF16), shape((64, SLOTS), F32), shape((SLOTS, 256), BF16)),
-        [pltpu.VMEM((64, REL_LANES), F32), pltpu.VMEM((128, 512), F32)],
+        (shape((512, 128), BF16), shape((64, SLOTS), F32)),
+        [pltpu.VMEM((SLOTS, 256), BF16), pltpu.VMEM((64, REL_LANES), F32), pltpu.VMEM((128, 512), F32)],
         flops=5_000_000_000,
     )(weights, features, index, weight)
     arrived = lax.all_to_all(message.reshape(NE, 8, 128), "ent", split_axis=0, concat_axis=0, tiled=True)
 
-    wide = shape((256, SLOTS), BF16)
-    tall = shape((SLOTS, SLOTS), BF16)
-    hots = shape((REL_PAD, SLOTS), BF16)
-    taken, src_hot, rel_hot = call(take_kernel, (tall, wide, hots), flops=4_000_000_000, vmem=24)(z, index)
     back, layer_t, grad_t = call(
         node_kernel,
         (shape((512, 128), BF16), shape((COL, 256), BF16), shape((COL, 256), BF16)),
@@ -354,28 +334,23 @@
     )(arrived.reshape(512, 128), index, features, self_t, out_grad.T)
     returned = lax.all_to_all(back.reshape(NE, 8, 128), "ent", split_axis=0, concat_axis=0, tiled=True)
 
-    grad_z, terms = call(
+    terms, input_t = call(
         grad_kernel,
-        (wide, shape((NE, G_TILES, 8, 128), BF16)),
+        (shape((NE, G_TILES, 8, 128), BF16), shape((256, 256), BF16)),
         [
-            pltpu.VMEM(tall.shape, BF16),
-            pltpu.VMEM((64, SLOTS), F32),
-            pltpu.VMEM(wide.shape, BF16),
-            pltpu.VMEM(hots.shape, BF16),
-            pltpu.VMEM((256, 256), BF16),
-            pltpu.VMEM(wide.shape, BF16),
+            pltpu.VMEM((SLOTS, 256), BF16),
+            pltpu.VMEM((SLOTS, 256), BF16),
+            pltpu.VMEM((256, SLOTS), BF16),
+            pltpu.VMEM((REL_PAD, SLOTS), BF16),
+            pltpu.VMEM((256, SLOTS), BF16),
             pltpu.VMEM((COL, SLOTS), F32),
-            pltpu.VMEM(tall.shape, BF16),
+            pltpu.VMEM((SLOTS, SLOTS), BF16),
             pltpu.VMEM((512, SLOTS), BF16),
-            pltpu.SemaphoreType.DMA((13,)),
         ],
         flops=8_000_000_000,
-        vmem=40,
-        places="hhhhh",
-        out_places="h",
-    )(taken, coef_slot, src_hot, rel_hot, features, returned.reshape(512, 128), weight, grad_t)
+        vmem=32,
+    )(returned.reshape(512, 128), weights, coef_slot, features, index, weight, self_t, grad_t)
     terms = lax.all_to_all(terms, "ent", split_axis=0, concat_axis=0, tiled=True)
-    input_t = call(input_kernel, shape((256, 256), BF16), flops=2_000_000_000)(grad_z, weights, grad_t, self_t)
 
     chunk, own = call(
         sum_kernel,

time: 196 us -> 173 us (0.88)
  blocking collectives: 64.5 us -> 120 us
  waiting for transfers between devices: 54.5 us -> 23.9 us
  starting transfers between devices: 28 us -> 7.83 us
  local copies, waits for them, and re-layouts: 17.5 us -> 0.65 us
  Pallas kernels: 28.8 us -> 18.6 us
    all_to_all x0 -> x2, blocking collectives: none -> 55 us  [the longest x1 38.3 us: body(): lax.all_to_all(terms, 'ent', split_axis=0, concat_axis=0, tiled=True)]
    all_to_all x2 -> x0, waiting for transfers between devices: 30.6 us -> none  [the longest x1 30.6 us: body(): lax.all_to_all(terms, 'ent', split_axis=0, concat_axis=0, tiled=True)]
    all_to_all x2 -> x0, starting transfers between devices: 20.2 us -> none  [the longest x1 12.8 us: body(): lax.all_to_all(terms, 'ent', split_axis=0, concat_axis=0, tiled=True)]
    unnamed x38 -> x16, local copies, waits for them, and re-layouts: 16.9 us -> 0.05 us
    pallas_call x9 -> x7, Pallas kernels: 28.8 us -> 18.6 us  [run(): pl.pallas_call(kernel, out_shape=outs, in_specs=[spec(places, n) for n in...]
  transfers between devices with their start and end apart: 4 -> 2, of which waited for: 3 -> 2; matrix products, arithmetic and copies ran while one was open for 0% -> 0% of each run, Pallas kernels for 3% -> 0%
where the time goes in v4:
time: 173 us; the launch traced here: 171 us
  blocking collectives  120 us (69%)
  waiting for transfers between devices  23.9 us (14%)
  Pallas kernels  18.6 us (11%)
  starting transfers between devices  7.83 us (5%)
    all_to_all x1, blocking collectives, body(): lax.all_to_all(merged, 'ent', split_axis=0, concat_axis=0, tiled=True)  39 us
    all_to_all x1, blocking collectives, body(): lax.all_to_all(terms, 'ent', split_axis=0, concat_axis=0, tiled=True)  38.3 us
    all_to_all x1, blocking collectives, body(): lax.all_to_all(message.reshape(NE, 8, 128), 'ent', split_axis=0, concat_a...  25.6 us
    pallas_call x7, Pallas kernels, run(): pl.pallas_call(kernel, out_shape=outs, in_specs=[spec(places, n) for n in...  18.6 us
    all_to_all x1, waiting for transfers between devices, body(): lax.all_to_all(payload, 'rel', split_axis=0, concat_axis=0, tiled=True)  17.3 us
    all_to_all x1, blocking collectives, body(): lax.all_to_all(back.reshape(NE, 8, 128), 'ent', split_axis=0, concat_axis...  16.7 us
    all_to_all x1, waiting for transfers between devices, body(): lax.all_to_all(chunk, 'rel', split_axis=0, concat_axis=0, tiled=True)  6.58 us
    all_to_all x1, starting transfers between devices, body(): lax.all_to_all(payload, 'rel', split_axis=0, concat_axis=0, tiled=True)  4.44 us
  transfers between devices with their start and end apart: 2, of which 2 were waited for; matrix products, arithmetic and copies ran while one was open for 0% of the time, Pallas kernels for 0%

profile of v4, /device:TPU:56, one launch (start us, length us, event | category | flops | bytes accessed | tf_op | source)
XLA Modules:
  0.0 171.3 jit_solution(7710442634978605184)
XLA Ops:
  0.6 2.6 %shard_map.137 = bf16[8,304,256]{2,1,0:T(8,128)(2,1)} custom-call(bf16[8,256,256]{2,1,0:T(8,128)(2,1)} %basis_ref.1, f32[8,1300]{1,0:T(8,128)} %bitcast.33), custom_call_target="tpu_custom_call" | custom-call | bytes 4194304 | tf_op jit(solution)/shard_map/pallas_call | solution.py:53
  3.2 0.0 copy-start.5
  3.3 0.0 copy-start.6
  3.3 0.0 copy-start.7
  3.3 4.4 %all-to-all-start = ((bf16[8,304,256]{2,1,0:T(8,128)(2,1)}), bf16[8,304,256]{2,1,0:T(8,128)(2,1)S(1)}, u32[]{:S(2)}, u32[]{:S(2)}) async-start(bf16[8,304,256]{2,1,0:T(8,128)(2,1)} %shard_map.137), calls=%async_computation | async-start | bytes 2490368 | tf_op jit(solution)/shard_map/all_to_all | solution.py:311
  7.8 0.2 copy.23
  8.0 0.2 reshape.39.index_ref
  8.2 0.1 copy.24
  8.3 0.1 reshape.40.weight_ref
  8.4 0.0 copy-start.1
  8.5 0.0 copy-start.2
  8.5 17.3 %all-to-all-done.w_ref = bf16[8,304,256]{2,1,0:T(8,128)(2,1)S(1)} async-done(((bf16[8,304,256]{2,1,0:T(8,128)(2,1)}), bf16[8,304,256]{2,1,0:T(8,128)(2,1)S(1)}, u32[]{:S(2)}, u32[]{:S(2)}) %all-to-all-start) | async-done | bytes 1245216 | tf_op jit(solution)/shard_map/all_to_all | solution.py:311
  25.8 4.0 %shard_map.138 = (bf16[512,128]{1,0:T(8,128)(2,1)S(1)}, f32[64,2048]{1,0:T(8,128)S(1)}) custom-call(bf16[8,304,256]{2,1,0:T(8,128)(2,1)S(1)} %all-to-all-done.w_ref, bf16[256,256]{1,0:T(8,128)(2,1)S(1)} %copy-done, s32[3,2048]{1,0:T(4,128)S(1)} %reshape.39.index_ref, f32[1,2048]{1,0:T(1,128)S(1)} %reshape.40.weight_ref), custom_call_target="tpu_custom_call" | custom-call | flops 5000000000 | bytes 4194304 | tf_op jit(solution)/shard_map/pallas_call | solution.py:53
  29.8 25.6 %all_to_all.30 = bf16[64,8,128]{2,1,0:T(8,128)(2,1)S(1)} all-to-all(bf16[64,8,128]{2,1,0:T(8,128)(2,1)S(1)} %bitcast.28), channel_id=1, replica_groups=mesh['ent'=64,'rel'=8] {'ent'}, dimensions={0} | all-to-all | bytes 262144 | tf_op jit(solution)/shard_map/all_to_all | solution.py:327
  55.4 1.4 shard_map.139
  56.8 16.7 %all_to_all.31 = bf16[64,8,128]{2,1,0:T(8,128)(2,1)S(1)} all-to-all(bf16[64,8,128]{2,1,0:T(8,128)(2,1)S(1)} %bitcast.27), channel_id=1, replica_groups=mesh['ent'=64,'rel'=8] {'ent'}, dimensions={0} | all-to-all | bytes 262144 | tf_op jit(solution)/shard_map/all_to_all | solution.py:335
  73.4 7.3 %shard_map.140 = (bf16[64,10,8,128]{3,2,1,0:T(8,128)(2,1)S(1)}, bf16[256,256]{1,0:T(8,128)(2,1)S(1)}) custom-call(bf16[512,128]{1,0:T(8,128)(2,1)S(1)} %bitcast.25, bf16[8,304,256]{2,1,0:T(8,128)(2,1)S(1)} %all-to-all-done.w_ref, f32[64,2048]{1,0:T(8,128)S(1)} %get-tuple-element.22.coef_ref, bf16[256,256]{1,0:T(8,128)(2,1)S(1)} %copy-done, ...), custom_call_target="tpu_custom_call" | custom-call | flops 8000000000 | bytes 4194304 | tf_op jit(solution)/shard_map/pallas_call | solution.py:53
  80.8 38.3 %all_to_all.32.got_ref = bf16[64,10,8,128]{3,2,1,0:T(8,128)(2,1)S(1)} all-to-all(bf16[64,10,8,128]{3,2,1,0:T(8,128)(2,1)S(1)} %get-tuple-element.24), channel_id=1, replica_groups=mesh['ent'=64,'rel'=8] {'ent'}, dimensions={0} | all-to-all | bytes 2621440 | tf_op jit(solution)/shard_map/all_to_all | solution.py:353
  119.1 0.9 shard_map.141
  120.0 3.4 %all-to-all-start.4 = ((bf16[8,11,8,128]{3,2,1,0:T(8,128)(2,1)}), bf16[8,11,8,128]{3,2,1,0:T(8,128)(2,1)S(1)}, u32[]{:S(2)}, u32[]{:S(2)}) async-start(bf16[8,11,8,128]{3,2,1,0:T(8,128)(2,1)} %get-tuple-element.26), calls=%async_computation.4 | async-start | bytes 360448 | tf_op jit(solution)/shard_map/all_to_all | solution.py:359
  123.4 6.6 %all-to-all-done.4.got_ref = bf16[8,11,8,128]{3,2,1,0:T(8,128)(2,1)S(1)} async-done(((bf16[8,11,8,128]{3,2,1,0:T(8,128)(2,1)}), bf16[8,11,8,128]{3,2,1,0:T(8,128)(2,1)S(1)}, u32[]{:S(2)}, u32[]{:S(2)}) %all-to-all-start.4) | async-done | bytes 180256 | tf_op jit(solution)/shard_map/all_to_all | solution.py:359
  129.9 0.8 shard_map.142
  130.7 39.0 %all_to_all.33.got_ref = bf16[64,9,8,128]{3,2,1,0:T(8,128)(2,1)S(1)} all-to-all(bf16[64,9,8,128]{3,2,1,0:T(8,128)(2,1)S(1)} %get-tuple-element.29), channel_id=1, replica_groups=mesh['ent'=64,'rel'=8] {'ent'}, dimensions={0} | all-to-all | bytes 2359296 | tf_op jit(solution)/shard_map/all_to_all | solution.py:366
  169.7 1.6 shard_map.143
  (13 shorter events, 0.0 us)
Async XLA Ops:
  3.2 4.5 %copy-start.4 = (s32[64,32]{0,1:T(8,128)S(1)}, s32[64,32]{0,1:T(8,128)}, u32[]{:S(2)}) copy-start(s32[64,32]{0,1:T(8,128)} %param.16) | copy-start | bytes 24580
  3.2 4.5 %copy-start.5 = (s32[64,32]{0,1:T(8,128)S(1)}, s32[64,32]{0,1:T(8,128)}, u32[]{:S(2)}) copy-start(s32[64,32]{0,1:T(8,128)} %param.15) | copy-start | bytes 24580
  3.3 4.5 %copy-start.6 = (s32[64,32]{0,1:T(8,128)S(1)}, s32[64,32]{0,1:T(8,128)}, u32[]{:S(2)}) copy-start(s32[64,32]{0,1:T(8,128)} %param.14) | copy-start | bytes 24580
  3.3 4.9 %copy-start.3 = (f32[64,32]{0,1:T(8,128)S(1)}, f32[64,32]{0,1:T(8,128)}, u32[]{:S(2)}) copy-start(f32[64,32]{0,1:T(8,128)} %param.17) | copy-start | bytes 24580
  3.3 4.9 %copy-start.7 = (s32[1,64]{1,0:T(1,128)S(1)}, s32[1,64]{1,0:T(1,128)}, u32[]{:S(2)}) copy-start(s32[1,64]{1,0:T(1,128)} %param.18) | copy-start | bytes 772
  3.3 22.5 %all-to-all-start = ((bf16[8,304,256]{2,1,0:T(8,128)(2,1)}), bf16[8,304,256]{2,1,0:T(8,128)(2,1)S(1)}, u32[]{:S(2)}, u32[]{:S(2)}) async-start(bf16[8,304,256]{2,1,0:T(8,128)(2,1)} %shard_map.137), calls=%async_computation | async-start | bytes 2490368 | tf_op jit(solution)/shard_map/all_to_all | solution.py:311
  7.7 18.1 %copy-start = (bf16[256,256]{1,0:T(8,128)(2,1)S(1)}, bf16[256,256]{1,0:T(8,128)(2,1)}, u32[]{:S(2)}) copy-start(bf16[256,256]{1,0:T(8,128)(2,1)} %x_ref.5) | copy-start | bytes 393220
  8.4 47.0 %copy-start.1 = (bf16[256,32]{0,1:T(8,128)(2,1)S(1)}, bf16[256,32]{0,1:T(8,128)(2,1)}, u32[]{:S(2)}) copy-start(bf16[256,32]{0,1:T(8,128)(2,1)} %param.19) | copy-start | bytes 49156
  8.5 47.0 %copy-start.2 = (bf16[256,32]{0,1:T(8,128)(2,1)S(1)}, bf16[256,32]{0,1:T(8,128)(2,1)}, u32[]{:S(2)}) copy-start(bf16[256,32]{0,1:T(8,128)(2,1)} %param.13) | copy-start | bytes 49156
  120.0 10.0 %all-to-all-start.4 = ((bf16[8,11,8,128]{3,2,1,0:T(8,128)(2,1)}), bf16[8,11,8,128]{3,2,1,0:T(8,128)(2,1)S(1)}, u32[]{:S(2)}, u32[]{:S(2)}) async-start(bf16[8,11,8,128]{3,2,1,0:T(8,128)(2,1)} %get-tuple-element.26), calls=%async_computation.4 | async-start | bytes 360448 | tf_op jit(solution)/shard_map/all_to_all | solution.py:359

commit v5 on v4

--- a/solution.py
+++ b/solution.py
@@ -10,6 +10,7 @@
 BF16 = jnp.bfloat16
 
 NE = 64
+SIDE = 8
 NK = 8
 GB = 8
 COL = 32
@@ -250,18 +251,26 @@
     rest = pltpu.roll(own_ref[...], 96, 1)
     tiles.append(jnp.where(lane < 8, first, jnp.where(lane < 16, second, jnp.where(lane < 32, third, rest))))
     chunk = jnp.stack(tiles).astype(BF16)
-
-    def copy(n, carry):
+    for n in range(SIDE):
         out_ref[n] = chunk
-        return carry
-
-    lax.fori_loop(0, NE, copy, 0, unroll=8)
-
-
-def finish_kernel(got_ref, basis_ref, coef_ref, self_ref, rel_ref, own_ref):
+
+
+def copy_kernel(got_ref, out_ref):
+    for n in range(SIDE):
+        for m in range(SIDE):
+            out_ref[n, m] = got_ref[m]
+
+
+def finish_kernel(core_ref, got_ref, basis_hbm, coef_ref, self_ref, basis_ref, rel_ref, own_ref, sems):
+    core = core_ref[0]
+    copies = []
+    for h in range(2):
+        place = pl.ds(h * 4, 4)
+        copies.append(pltpu.make_async_copy(basis_ref.at[place], basis_hbm.at[place], sems.at[h]))
     for n in range(NE):
+        z, y = divmod(n, SIDE)
         h, ib = divmod(n, 32)
-        part = got_ref[n].astype(F32)
+        part = got_ref[n + core * (y * SIDE + z - n)].astype(F32)
         for l in range(4):
             for o in range(2):
                 basis_ref[h * 4 + l, ib * 8 : ib * 8 + 8, o * 128 : o * 128 + 128] = part[l * 2 + o]
@@ -271,11 +280,35 @@
                 rel_ref[n * REL_CHUNK + t * 8 : n * REL_CHUNK + t * 8 + 8, :] = piece
         if n < 32:
             own_ref[n * 8 : n * 8 + 8, :] = pltpu.roll(part[8], 96, 1)
+        if ib == 31:
+            copies[h].start()
     for t in range(11):
         across = rel_ref[t * 128 : (t + 1) * 128, :].T[0:8, :]
         width = min(128, RELS - t * 128)
         coef_ref[:, t * 128 : t * 128 + width] = across[:, 0:width]
     self_ref[...] = own_ref[...].T[0:32, :]
+    for copy in copies:
+        copy.wait()
+
+
+def lines(first):
+    def place(z, y, rel):
+        return (z * SIDE + y) * NK + rel
+
+    groups = []
+    for rel in range(NK):
+        for a in range(SIDE):
+            if rel % 2 == first:
+                groups.append([place(a, b, rel) for b in range(SIDE)])
+            else:
+                groups.append([place(b, a, rel) for b in range(SIDE)])
+    return groups
+
+
+def line_exchange(a, first):
+    return lax.all_to_all(
+        a, ("ent", "rel"), split_axis=0, concat_axis=0, axis_index_groups=lines(first), tiled=True
+    )
 
 
 def body(
@@ -360,16 +393,25 @@
 
     merged, input_grad_t = call(
         merge_kernel,
-        (shape((NE, F_TILES, 8, 128), BF16), shape((COL, 256), F32)),
+        (shape((SIDE, F_TILES, 8, 128), BF16), shape((COL, 256), F32)),
         places="s",
     )(me, chunk, own)
-    gathered = lax.all_to_all(merged, "ent", split_axis=0, concat_axis=0, tiled=True)
+    line = line_exchange(merged, 0)
+    copied = call(copy_kernel, shape((SIDE, SIDE, F_TILES, 8, 128), BF16))(line)
+    gathered = line_exchange(copied, 1).reshape(NE, F_TILES, 8, 128)
 
     basis_grad, coef_t, self_grad_t = call(
         finish_kernel,
         (shape((GB, 256, 256), F32), shape((GB, RELS), F32), shape((COL, 256), F32)),
-        [pltpu.VMEM((11 * 128, 128), F32), pltpu.VMEM((256, 128), F32)],
-    )(gathered)
+        [
+            pltpu.VMEM((GB, 256, 256), F32),
+            pltpu.VMEM((11 * 128, 128), F32),
+            pltpu.VMEM((256, 128), F32),
+            pltpu.SemaphoreType.DMA((2,)),
+        ],
+        places="s",
+        out_places="h",
+    )(lax.rem(me, 2), gathered)
     return (layer_t.T, input_grad_t.T, coef_t.T, basis_grad, self_grad_t.T)
 
 

time: 173 us -> 173 us (level)
  blocking collectives: 120 us -> 92.3 us
  waiting for transfers between devices: 23.9 us -> 44.2 us
  starting transfers between devices: 7.83 us -> 11.4 us
    all_to_all x1, blocking collectives: 39 us -> 11.8 us  [line_exchange(): lax.all_to_all(a, ('ent', 'rel'), split_axis=0, concat_axis=0, axis_index...]
    all_to_all x0 -> x1, waiting for transfers between devices: none -> 20.3 us  [line_exchange(): lax.all_to_all(a, ('ent', 'rel'), split_axis=0, concat_axis=0, axis_index...]
    all_to_all x0 -> x1, starting transfers between devices: none -> 3.56 us  [line_exchange(): lax.all_to_all(a, ('ent', 'rel'), split_axis=0, concat_axis=0, axis_index...]
    pallas_call x7 -> x8, Pallas kernels: 18.6 us -> 20.2 us  [run(): pl.pallas_call(kernel, out_shape=outs, in_specs=[spec(places, n) for n in...]
  transfers between devices with their start and end apart: 2 -> 3, of which waited for: 2 -> 3; matrix products, arithmetic and copies ran while one was open for 0% -> 0% of each run, Pallas kernels for 0% -> 0%
where the time goes in v5:
time: 173 us; the launch traced here: 170 us
  blocking collectives  92.3 us (53%)
  waiting for transfers between devices  44.2 us (26%)
  Pallas kernels  20.2 us (12%)
  starting transfers between devices  11.4 us (7%)
    all_to_all x1, blocking collectives, body(): lax.all_to_all(terms, 'ent', split_axis=0, concat_axis=0, tiled=True)  38.3 us
    all_to_all x1, blocking collectives, body(): lax.all_to_all(message.reshape(NE, 8, 128), 'ent', split_axis=0, concat_a...  25.6 us
    all_to_all x1, waiting for transfers between devices, line_exchange(): lax.all_to_all(a, ('ent', 'rel'), split_axis=0, concat_axis=0, axis_index...  20.3 us
    pallas_call x8, Pallas kernels, run(): pl.pallas_call(kernel, out_shape=outs, in_specs=[spec(places, n) for n in...  20.2 us
    all_to_all x1, waiting for transfers between devices, body(): lax.all_to_all(payload, 'rel', split_axis=0, concat_axis=0, tiled=True)  17.3 us
    all_to_all x1, blocking collectives, body(): lax.all_to_all(back.reshape(NE, 8, 128), 'ent', split_axis=0, concat_axis...  16.7 us
    all_to_all x1, blocking collectives, line_exchange(): lax.all_to_all(a, ('ent', 'rel'), split_axis=0, concat_axis=0, axis_index...  11.8 us
    all_to_all x1, waiting for transfers between devices, body(): lax.all_to_all(chunk, 'rel', split_axis=0, concat_axis=0, tiled=True)  6.58 us
  transfers between devices with their start and end apart: 3, of which 3 were waited for; matrix products, arithmetic and copies ran while one was open for 0% of the time, Pallas kernels for 0%

profile of v5, /device:TPU:56, one launch (start us, length us, event | category | flops | bytes accessed | tf_op | source)
XLA Modules:
  0.0 169.7 jit_solution(363210823419669172)
XLA Ops:
  0.6 2.6 %shard_map.137 = bf16[8,304,256]{2,1,0:T(8,128)(2,1)} custom-call(bf16[8,256,256]{2,1,0:T(8,128)(2,1)} %basis_ref.1, f32[8,1300]{1,0:T(8,128)} %bitcast.35), custom_call_target="tpu_custom_call" | custom-call | bytes 4194304 | tf_op jit(solution)/shard_map/pallas_call | solution.py:54
  3.3 0.0 copy-start.6
  3.3 0.0 copy-start.3
  3.3 4.4 %all-to-all-start = ((bf16[8,304,256]{2,1,0:T(8,128)(2,1)}), bf16[8,304,256]{2,1,0:T(8,128)(2,1)S(1)}, u32[]{:S(2)}, u32[]{:S(2)}) async-start(bf16[8,304,256]{2,1,0:T(8,128)(2,1)} %shard_map.137), calls=%async_computation | async-start | bytes 2490368 | tf_op jit(solution)/shard_map/all_to_all | solution.py:344
  7.8 0.2 copy.23
  8.0 0.2 reshape.44.index_ref
  8.2 0.1 copy.24
  8.3 0.1 reshape.45.weight_ref
  8.5 17.3 %all-to-all-done.w_ref = bf16[8,304,256]{2,1,0:T(8,128)(2,1)S(1)} async-done(((bf16[8,304,256]{2,1,0:T(8,128)(2,1)}), bf16[8,304,256]{2,1,0:T(8,128)(2,1)S(1)}, u32[]{:S(2)}, u32[]{:S(2)}) %all-to-all-start) | async-done | bytes 1245216 | tf_op jit(solution)/shard_map/all_to_all | solution.py:344
  25.8 4.0 %shard_map.138 = (bf16[512,128]{1,0:T(8,128)(2,1)S(1)}, f32[64,2048]{1,0:T(8,128)S(1)}) custom-call(bf16[8,304,256]{2,1,0:T(8,128)(2,1)S(1)} %all-to-all-done.w_ref, bf16[256,256]{1,0:T(8,128)(2,1)S(1)} %copy-done, s32[3,2048]{1,0:T(4,128)S(1)} %reshape.44.index_ref, f32[1,2048]{1,0:T(1,128)S(1)} %reshape.45.weight_ref), custom_call_target="tpu_custom_call" | custom-call | flops 5000000000 | bytes 4194304 | tf_op jit(solution)/shard_map/pallas_call | solution.py:54
  29.8 25.6 %all_to_all.35 = bf16[64,8,128]{2,1,0:T(8,128)(2,1)S(1)} all-to-all(bf16[64,8,128]{2,1,0:T(8,128)(2,1)S(1)} %bitcast.30), channel_id=1, replica_groups=mesh['ent'=64,'rel'=8] {'ent'}, dimensions={0} | all-to-all | bytes 262144 | tf_op jit(solution)/shard_map/all_to_all | solution.py:360
  55.4 1.4 shard_map.139
  56.8 16.7 %all_to_all.36 = bf16[64,8,128]{2,1,0:T(8,128)(2,1)S(1)} all-to-all(bf16[64,8,128]{2,1,0:T(8,128)(2,1)S(1)} %bitcast.29), channel_id=1, replica_groups=mesh['ent'=64,'rel'=8] {'ent'}, dimensions={0} | all-to-all | bytes 262144 | tf_op jit(solution)/shard_map/all_to_all | solution.py:368
  73.4 7.3 %shard_map.140 = (bf16[64,10,8,128]{3,2,1,0:T(8,128)(2,1)S(1)}, bf16[256,256]{1,0:T(8,128)(2,1)S(1)}) custom-call(bf16[512,128]{1,0:T(8,128)(2,1)S(1)} %bitcast.27, bf16[8,304,256]{2,1,0:T(8,128)(2,1)S(1)} %all-to-all-done.w_ref, f32[64,2048]{1,0:T(8,128)S(1)} %get-tuple-element.22.coef_ref, bf16[256,256]{1,0:T(8,128)(2,1)S(1)} %copy-done, ...), custom_call_target="tpu_custom_call" | custom-call | flops 8000000000 | bytes 4194304 | tf_op jit(solution)/shard_map/pallas_call | solution.py:54
  80.8 38.3 %all_to_all.37.got_ref = bf16[64,10,8,128]{3,2,1,0:T(8,128)(2,1)S(1)} all-to-all(bf16[64,10,8,128]{3,2,1,0:T(8,128)(2,1)S(1)} %get-tuple-element.24), channel_id=1, replica_groups=mesh['ent'=64,'rel'=8] {'ent'}, dimensions={0} | all-to-all | bytes 2621440 | tf_op jit(solution)/shard_map/all_to_all | solution.py:386
  119.1 0.9 shard_map.141
  120.0 3.4 %all-to-all-start.4 = ((bf16[8,11,8,128]{3,2,1,0:T(8,128)(2,1)}), bf16[8,11,8,128]{3,2,1,0:T(8,128)(2,1)S(1)}, u32[]{:S(2)}, u32[]{:S(2)}) async-start(bf16[8,11,8,128]{3,2,1,0:T(8,128)(2,1)} %get-tuple-element.26), calls=%async_computation.4 | async-start | bytes 360448 | tf_op jit(solution)/shard_map/all_to_all | solution.py:392
  123.4 6.6 %all-to-all-done.4.got_ref = bf16[8,11,8,128]{3,2,1,0:T(8,128)(2,1)S(1)} async-done(((bf16[8,11,8,128]{3,2,1,0:T(8,128)(2,1)}), bf16[8,11,8,128]{3,2,1,0:T(8,128)(2,1)S(1)}, u32[]{:S(2)}, u32[]{:S(2)}) %all-to-all-start.4) | async-done | bytes 180256 | tf_op jit(solution)/shard_map/all_to_all | solution.py:392
  129.9 0.6 shard_map.142
  130.6 11.8 %all_to_all.38.got_ref = bf16[8,9,8,128]{3,2,1,0:T(8,128)(2,1)S(1)} all-to-all(bf16[8,9,8,128]{3,2,1,0:T(8,128)(2,1)S(1)} %get-tuple-element.29), channel_id=1, replica_groups={{0,8,16,24,32,40,48,56},{64,72,80,88,96,104,112,120},{128,136,144,152,1..., dimensions={0} | all-to-all | bytes 294912 | tf_op jit(solution)/shard_map/all_to_all | solution.py:309
  142.4 1.2 shard_map.143
  143.5 3.6 %all-to-all-start.6 = ((bf16[8,8,9,8,128]{4,3,2,1,0:T(8,128)(2,1)}), bf16[8,8,9,8,128]{4,3,2,1,0:T(8,128)(2,1)S(1)}, u32[]{:S(2)}, u32[]{:S(2)}) async-start(bf16[8,8,9,8,128]{4,3,2,1,0:T(8,128)(2,1)} %shard_map.143), calls=%async_computation.6 | async-start | bytes 2359296 | tf_op jit(solution)/shard_map/all_to_all | solution.py:309
  147.1 20.3 %all-to-all-done.6 = bf16[8,8,9,8,128]{4,3,2,1,0:T(8,128)(2,1)S(1)} async-done(((bf16[8,8,9,8,128]{4,3,2,1,0:T(8,128)(2,1)}), bf16[8,8,9,8,128]{4,3,2,1,0:T(8,128)(2,1)S(1)}, u32[]{:S(2)}, u32[]{:S(2)}) %all-to-all-start.6) | async-done | bytes 1179680 | tf_op jit(solution)/shard_map/all_to_all | solution.py:309
  167.4 2.2 %shard_map.144 = (f32[8,256,256]{2,1,0:T(8,128)}, f32[8,1300]{1,0:T(8,128)}, f32[32,256]{1,0:T(8,128)}) custom-call(s32[1]{0:T(128)S(6)} %rem.18.core_ref, bf16[64,9,8,128]{3,2,1,0:T(8,128)(2,1)S(1)} %bitcast.26), custom_call_target="tpu_custom_call" | custom-call | bytes 4194304 | tf_op jit(solution)/shard_map/pallas_call | solution.py:54
  (16 shorter events, 0.1 us)
Async XLA Ops:
  3.2 4.5 %copy-start.4 = (s32[64,32]{0,1:T(8,128)S(1)}, s32[64,32]{0,1:T(8,128)}, u32[]{:S(2)}) copy-start(s32[64,32]{0,1:T(8,128)} %param.16) | copy-start | bytes 24580
  3.2 4.5 %copy-start.5 = (s32[64,32]{0,1:T(8,128)S(1)}, s32[64,32]{0,1:T(8,128)}, u32[]{:S(2)}) copy-start(s32[64,32]{0,1:T(8,128)} %param.15) | copy-start | bytes 24580
  3.3 4.5 %copy-start.6 = (s32[64,32]{0,1:T(8,128)S(1)}, s32[64,32]{0,1:T(8,128)}, u32[]{:S(2)}) copy-start(s32[64,32]{0,1:T(8,128)} %param.14) | copy-start | bytes 24580
  3.3 4.9 %copy-start.3 = (f32[64,32]{0,1:T(8,128)S(1)}, f32[64,32]{0,1:T(8,128)}, u32[]{:S(2)}) copy-start(f32[64,32]{0,1:T(8,128)} %param.17) | copy-start | bytes 24580
  3.3 4.9 %copy-start.7 = (s32[1,64]{1,0:T(1,128)S(1)}, s32[1,64]{1,0:T(1,128)}, u32[]{:S(2)}) copy-start(s32[1,64]{1,0:T(1,128)} %param.18) | copy-start | bytes 772
  3.3 22.5 %all-to-all-start = ((bf16[8,304,256]{2,1,0:T(8,128)(2,1)}), bf16[8,304,256]{2,1,0:T(8,128)(2,1)S(1)}, u32[]{:S(2)}, u32[]{:S(2)}) async-start(bf16[8,304,256]{2,1,0:T(8,128)(2,1)} %shard_map.137), calls=%async_computation | async-start | bytes 2490368 | tf_op jit(solution)/shard_map/all_to_all | solution.py:344
  7.7 18.1 %copy-start = (bf16[256,256]{1,0:T(8,128)(2,1)S(1)}, bf16[256,256]{1,0:T(8,128)(2,1)}, u32[]{:S(2)}) copy-start(bf16[256,256]{1,0:T(8,128)(2,1)} %x_ref.5) | copy-start | bytes 393220
  8.4 47.0 %copy-start.1 = (bf16[256,32]{0,1:T(8,128)(2,1)S(1)}, bf16[256,32]{0,1:T(8,128)(2,1)}, u32[]{:S(2)}) copy-start(bf16[256,32]{0,1:T(8,128)(2,1)} %param.19) | copy-start | bytes 49156
  8.5 47.0 %copy-start.2 = (bf16[256,32]{0,1:T(8,128)(2,1)S(1)}, bf16[256,32]{0,1:T(8,128)(2,1)}, u32[]{:S(2)}) copy-start(bf16[256,32]{0,1:T(8,128)(2,1)} %param.13) | copy-start | bytes 49156
  120.0 10.0 %all-to-all-start.4 = ((bf16[8,11,8,128]{3,2,1,0:T(8,128)(2,1)}), bf16[8,11,8,128]{3,2,1,0:T(8,128)(2,1)S(1)}, u32[]{:S(2)}, u32[]{:S(2)}) async-start(bf16[8,11,8,128]{3,2,1,0:T(8,128)(2,1)} %get-tuple-element.26), calls=%async_computation.4 | async-start | bytes 360448 | tf_op jit(solution)/shard_map/all_to_all | solution.py:392
  143.5 23.8 %all-to-all-start.6 = ((bf16[8,8,9,8,128]{4,3,2,1,0:T(8,128)(2,1)}), bf16[8,8,9,8,128]{4,3,2,1,0:T(8,128)(2,1)S(1)}, u32[]{:S(2)}, u32[]{:S(2)}) async-start(bf16[8,8,9,8,128]{4,3,2,1,0:T(8,128)(2,1)} %shard_map.143), calls=%async_computation.6 | async-start | bytes 2359296 | tf_op jit(solution)/shard_map/all_to_all | solution.py:309

commit v6 on v4

--- a/solution.py
+++ b/solution.py
@@ -21,7 +21,7 @@
 BLK = 256
 W_ROWS = 304
 G_TILES = 10
-X_TILES = 11
+X_TILES = 3
 F_TILES = 9
 
 
@@ -38,8 +38,8 @@
 
 
 def hot(rows, index):
-    place = lax.broadcasted_iota(jnp.int32, (rows, index.shape[1]), 0)
-    return jnp.where(place == index, 1.0, 0.0).astype(BF16)
+    place = lax.broadcasted_iota(jnp.int16, (rows, index.shape[1]), 0)
+    return jnp.where(place == index.astype(jnp.int16), jnp.bfloat16(1), jnp.bfloat16(0))
 
 
 def call(kernel, out_shape, scratch=(), flops=0, vmem=16, places="", out_places=""):
@@ -204,10 +204,10 @@
         out_ref[n, 8] = jnp.where(left, first, third).astype(BF16)
         out_ref[n, 9] = jnp.where(left, second, rest).astype(BF16)
     total = tn(grad_ref[...], self_ref[...]) + nn(grad_z_ref[...], w_all[...])
-    input_ref[...] = total.T.astype(BF16)
-
-
-def sum_kernel(got_ref, input_ref, out_ref, own_ref):
+    input_ref[...] = total.T
+
+
+def sum_kernel(got_ref, out_ref, own_ref):
     def add(n, total):
         return total + got_ref[n].astype(F32)
 
@@ -215,24 +215,17 @@
     own_ref[...] = total[9]
     slab = total[8:10].astype(BF16)
     for k in range(NK):
-        for h in range(2):
-            part = input_ref[k * COL : (k + 1) * COL, h * 128 : h * 128 + 128]
-            out_ref[k, h * 4 : h * 4 + 4] = part.reshape(4, 8, 128)
-        out_ref[k, 8] = total[k].astype(BF16)
-        out_ref[k, 9:11] = slab
-
-
-def merge_kernel(me_ref, got_ref, own_ref, out_ref, input_ref):
+        out_ref[k, 0] = total[k].astype(BF16)
+        out_ref[k, 1:3] = slab
+
+
+def merge_kernel(me_ref, got_ref, own_ref, out_ref):
     me = me_ref[0]
-    total = got_ref[0, 0:8].astype(F32)
-    slab = got_ref[0, 9:11].astype(F32)
-    pieces = [got_ref[0, 8].astype(F32)]
+    slab = got_ref[0, 1:3].astype(F32)
+    pieces = [got_ref[0, 0].astype(F32)]
     for k in range(1, NK):
-        total += got_ref[k, 0:8].astype(F32)
-        slab += got_ref[k, 9:11].astype(F32)
-        pieces.append(got_ref[k, 8].astype(F32))
-    input_ref[:, 0:128] = total[0:4].reshape(32, 128)
-    input_ref[:, 128:256] = total[4:8].reshape(32, 128)
+        slab += got_ref[k, 1:3].astype(F32)
+        pieces.append(got_ref[k, 0].astype(F32))
     lane = lax.broadcasted_iota(jnp.int32, (8, 128), 1)
     tiles = []
     for l in range(4):
@@ -336,7 +329,7 @@
 
     terms, input_t = call(
         grad_kernel,
-        (shape((NE, G_TILES, 8, 128), BF16), shape((256, 256), BF16)),
+        (shape((NE, G_TILES, 8, 128), BF16), shape((256, 256), F32)),
         [
             pltpu.VMEM((SLOTS, 256), BF16),
             pltpu.VMEM((SLOTS, 256), BF16),
@@ -350,19 +343,16 @@
         flops=8_000_000_000,
         vmem=32,
     )(returned.reshape(512, 128), weights, coef_slot, features, index, weight, self_t, grad_t)
+    input_grad_t = lax.psum_scatter(input_t, "rel", scatter_dimension=0, tiled=True)
     terms = lax.all_to_all(terms, "ent", split_axis=0, concat_axis=0, tiled=True)
 
     chunk, own = call(
         sum_kernel,
         (shape((NK, X_TILES, 8, 128), BF16), shape((8, 128), F32)),
-    )(terms, input_t)
+    )(terms)
     chunk = lax.all_to_all(chunk, "rel", split_axis=0, concat_axis=0, tiled=True)
 
-    merged, input_grad_t = call(
-        merge_kernel,
-        (shape((NE, F_TILES, 8, 128), BF16), shape((COL, 256), F32)),
-        places="s",
-    )(me, chunk, own)
+    merged = call(merge_kernel, shape((NE, F_TILES, 8, 128), BF16), places="s")(me, chunk, own)
     gathered = lax.all_to_all(merged, "ent", split_axis=0, concat_axis=0, tiled=True)
 
     basis_grad, coef_t, self_grad_t = call(

time: 173 us -> 192 us (1.11)
  blocking collectives: 120 us -> 80.5 us
  waiting for transfers between devices: 23.9 us -> 60.4 us
  between operations: 0.8 us -> 14.2 us
  starting transfers between devices: 7.83 us -> 15.7 us
    all_to_all x1 -> x0, blocking collectives: 39 us -> none  [body(): lax.all_to_all(merged, 'ent', split_axis=0, concat_axis=0, tiled=True)]
    all_to_all x0 -> x1, waiting for transfers between devices: none -> 30.7 us  [body(): lax.all_to_all(merged, 'ent', split_axis=0, concat_axis=0, tiled=True)]
    all_to_all x0 -> x1, starting transfers between devices: none -> 7.88 us  [body(): lax.all_to_all(merged, 'ent', split_axis=0, concat_axis=0, tiled=True)]
    reduce_scatter x0 -> x1, waiting for transfers between devices: none -> 6.2 us  [body(): lax.psum_scatter(input_t, 'rel', scatter_dimension=0, tiled=True)]
  transfers between devices with their start and end apart: 2 -> 4, of which waited for: 2 -> 4; matrix products, arithmetic and copies ran while one was open for 0% -> 0% of each run, Pallas kernels for 0% -> 1%
where the time goes in v6:
time: 192 us; the launch traced here: 191 us
  blocking collectives  80.5 us (42%)
  waiting for transfers between devices  60.4 us (31%)
  Pallas kernels  19.3 us (10%)
  starting transfers between devices  15.7 us (8%)
  between operations  14.2 us (7%)
    all_to_all x1, blocking collectives, body(): lax.all_to_all(terms, 'ent', split_axis=0, concat_axis=0, tiled=True)  38.3 us
    all_to_all x1, waiting for transfers between devices, body(): lax.all_to_all(merged, 'ent', split_axis=0, concat_axis=0, tiled=True)  30.7 us
    all_to_all x1, blocking collectives, body(): lax.all_to_all(message.reshape(NE, 8, 128), 'ent', split_axis=0, concat_a...  25.6 us
    pallas_call x7, Pallas kernels, run(): pl.pallas_call(kernel, out_shape=outs, in_specs=[spec(places, n) for n in...  19.3 us
    all_to_all x1, waiting for transfers between devices, body(): lax.all_to_all(payload, 'rel', split_axis=0, concat_axis=0, tiled=True)  17.3 us
    all_to_all x1, blocking collectives, body(): lax.all_to_all(back.reshape(NE, 8, 128), 'ent', split_axis=0, concat_axis...  16.7 us
    all_to_all x1, starting transfers between devices, body(): lax.all_to_all(merged, 'ent', split_axis=0, concat_axis=0, tiled=True)  7.88 us
    reduce_scatter x1, waiting for transfers between devices, body(): lax.psum_scatter(input_t, 'rel', scatter_dimension=0, tiled=True)  6.2 us
  transfers between devices with their start and end apart: 4, of which 4 were waited for; matrix products, arithmetic and copies ran while one was open for 0% of the time, Pallas kernels for 1%

profile of v6, /device:TPU:56, one launch (start us, length us, event | category | flops | bytes accessed | tf_op | source)
XLA Modules:
  0.0 190.8 jit_solution(16387115528302275736)
XLA Ops:
  7.2 2.6 %shard_map.137 = bf16[8,304,256]{2,1,0:T(8,128)(2,1)} custom-call(bf16[8,256,256]{2,1,0:T(8,128)(2,1)} %basis_ref.1, f32[8,1300]{1,0:T(8,128)} %bitcast.33), custom_call_target="tpu_custom_call" | custom-call | bytes 4194304 | tf_op jit(solution)/shard_map/pallas_call | solution.py:53
  9.8 0.0 copy-start.4
  9.8 4.4 %all-to-all-start = ((bf16[8,304,256]{2,1,0:T(8,128)(2,1)}), bf16[8,304,256]{2,1,0:T(8,128)(2,1)S(1)}, u32[]{:S(2)}, u32[]{:S(2)}) async-start(bf16[8,304,256]{2,1,0:T(8,128)(2,1)} %shard_map.137), calls=%async_computation | async-start | bytes 2490368 | tf_op jit(solution)/shard_map/all_to_all | solution.py:304
  14.3 0.2 copy.23
  14.5 0.2 reshape.39.index_ref
  14.8 0.1 copy.24
  14.9 0.1 reshape.40.weight_ref
  15.0 17.3 %all-to-all-done.w_ref = bf16[8,304,256]{2,1,0:T(8,128)(2,1)S(1)} async-done(((bf16[8,304,256]{2,1,0:T(8,128)(2,1)}), bf16[8,304,256]{2,1,0:T(8,128)(2,1)S(1)}, u32[]{:S(2)}, u32[]{:S(2)}) %all-to-all-start) | async-done | bytes 1245216 | tf_op jit(solution)/shard_map/all_to_all | solution.py:304
  32.3 3.8 %shard_map.138 = (bf16[512,128]{1,0:T(8,128)(2,1)S(1)}, f32[64,2048]{1,0:T(8,128)S(1)}) custom-call(bf16[8,304,256]{2,1,0:T(8,128)(2,1)S(1)} %all-to-all-done.w_ref, bf16[256,256]{1,0:T(8,128)(2,1)S(1)} %copy-done, s32[3,2048]{1,0:T(4,128)S(1)} %reshape.39.index_ref, f32[1,2048]{1,0:T(1,128)S(1)} %reshape.40.weight_ref), custom_call_target="tpu_custom_call" | custom-call | flops 5000000000 | bytes 4194304 | tf_op jit(solution)/shard_map/pallas_call | solution.py:53
  36.1 25.6 %all_to_all.30 = bf16[64,8,128]{2,1,0:T(8,128)(2,1)S(1)} all-to-all(bf16[64,8,128]{2,1,0:T(8,128)(2,1)S(1)} %bitcast.28), channel_id=1, replica_groups=mesh['ent'=64,'rel'=8] {'ent'}, dimensions={0} | all-to-all | bytes 262144 | tf_op jit(solution)/shard_map/all_to_all | solution.py:320
  61.7 1.4 shard_map.139
  63.1 16.7 %all_to_all.31 = bf16[64,8,128]{2,1,0:T(8,128)(2,1)S(1)} all-to-all(bf16[64,8,128]{2,1,0:T(8,128)(2,1)S(1)} %bitcast.27), channel_id=1, replica_groups=mesh['ent'=64,'rel'=8] {'ent'}, dimensions={0} | all-to-all | bytes 262144 | tf_op jit(solution)/shard_map/all_to_all | solution.py:328
  79.7 7.9 %shard_map.140 = (bf16[64,10,8,128]{3,2,1,0:T(8,128)(2,1)S(1)}, f32[256,256]{1,0:T(8,128)}) custom-call(bf16[512,128]{1,0:T(8,128)(2,1)S(1)} %bitcast.25, bf16[8,304,256]{2,1,0:T(8,128)(2,1)S(1)} %all-to-all-done.w_ref, f32[64,2048]{1,0:T(8,128)S(1)} %get-tuple-element.20.coef_ref, bf16[256,256]{1,0:T(8,128)(2,1)S(1)} %copy-done, ...), custom_call_target="tpu_custom_call" | custom-call | flops 8000000000 | bytes 4194304 | tf_op jit(solution)/shard_map/pallas_call | solution.py:53
  87.7 38.3 %all_to_all.32.got_ref = bf16[64,10,8,128]{3,2,1,0:T(8,128)(2,1)S(1)} all-to-all(bf16[64,10,8,128]{3,2,1,0:T(8,128)(2,1)S(1)} %get-tuple-element.23), channel_id=1, replica_groups=mesh['ent'=64,'rel'=8] {'ent'}, dimensions={0} | all-to-all | bytes 2621440 | tf_op jit(solution)/shard_map/all_to_all | solution.py:347
  125.9 0.8 shard_map.141
  126.8 3.3 %all-to-all-start.4 = ((bf16[8,3,8,128]{3,2,1,0:T(8,128)(2,1)}), bf16[8,3,8,128]{3,2,1,0:T(8,128)(2,1)S(1)}, u32[]{:S(2)}, u32[]{:S(2)}) async-start(bf16[8,3,8,128]{3,2,1,0:T(8,128)(2,1)} %get-tuple-element.24), calls=%async_computation.5 | async-start | bytes 98304 | tf_op jit(solution)/shard_map/all_to_all | solution.py:353
  130.1 5.4 %all-to-all-done.4.got_ref = bf16[8,3,8,128]{3,2,1,0:T(8,128)(2,1)S(1)} async-done(((bf16[8,3,8,128]{3,2,1,0:T(8,128)(2,1)}), bf16[8,3,8,128]{3,2,1,0:T(8,128)(2,1)S(1)}, u32[]{:S(2)}, u32[]{:S(2)}) %all-to-all-start.4) | async-done | bytes 49184 | tf_op jit(solution)/shard_map/all_to_all | solution.py:353
  135.6 1.2 shard_map.142
  136.8 7.9 %all-to-all-start.5 = ((bf16[64,9,8,128]{3,2,1,0:T(8,128)(2,1)}), bf16[64,9,8,128]{3,2,1,0:T(8,128)(2,1)S(1)}, u32[]{:S(2)}, u32[]{:S(2)}) async-start(bf16[64,9,8,128]{3,2,1,0:T(8,128)(2,1)} %shard_map.142), calls=%async_computation.6 | async-start | bytes 2359296 | tf_op jit(solution)/shard_map/all_to_all | solution.py:356
  144.7 0.0 reduce-scatter.2.cloned.1.call-start
  144.7 0.7 reduce-scatter.2.cloned.1.call-update
  145.4 30.7 %all-to-all-done.5.got_ref = bf16[64,9,8,128]{3,2,1,0:T(8,128)(2,1)S(1)} async-done(((bf16[64,9,8,128]{3,2,1,0:T(8,128)(2,1)}), bf16[64,9,8,128]{3,2,1,0:T(8,128)(2,1)S(1)}, u32[]{:S(2)}, u32[]{:S(2)}) %all-to-all-start.5) | async-done | bytes 1179680 | tf_op jit(solution)/shard_map/all_to_all | solution.py:356
  176.1 1.6 shard_map.143
  177.8 6.2 %reduce-scatter.2.cloned.1.call-done = f32[32,256]{1,0:T(8,128)} async-done(((f32[256,256]{1,0:T(8,128)}), f32[32,256]{1,0:T(8,128)}) %reduce-scatter.2.cloned.1.call-update) | async-done | bytes 32784 | tf_op jit(solution)/shard_map/reduce_scatter | solution.py:346
  (17 shorter events, 0.1 us)
Async XLA Ops:
  9.8 4.5 %copy-start.4 = (s32[64,32]{0,1:T(8,128)S(1)}, s32[64,32]{0,1:T(8,128)}, u32[]{:S(2)}) copy-start(s32[64,32]{0,1:T(8,128)} %param.16) | copy-start | bytes 24580
  9.8 4.5 %copy-start.5 = (s32[64,32]{0,1:T(8,128)S(1)}, s32[64,32]{0,1:T(8,128)}, u32[]{:S(2)}) copy-start(s32[64,32]{0,1:T(8,128)} %param.15) | copy-start | bytes 24580
  9.8 4.5 %copy-start.6 = (s32[64,32]{0,1:T(8,128)S(1)}, s32[64,32]{0,1:T(8,128)}, u32[]{:S(2)}) copy-start(s32[64,32]{0,1:T(8,128)} %param.14) | copy-start | bytes 24580
  9.8 4.9 %copy-start.3 = (f32[64,32]{0,1:T(8,128)S(1)}, f32[64,32]{0,1:T(8,128)}, u32[]{:S(2)}) copy-start(f32[64,32]{0,1:T(8,128)} %param.17) | copy-start | bytes 24580
  9.8 4.9 %copy-start.7 = (s32[1,64]{1,0:T(1,128)S(1)}, s32[1,64]{1,0:T(1,128)}, u32[]{:S(2)}) copy-start(s32[1,64]{1,0:T(1,128)} %param.18) | copy-start | bytes 772
  9.8 22.5 %all-to-all-start = ((bf16[8,304,256]{2,1,0:T(8,128)(2,1)}), bf16[8,304,256]{2,1,0:T(8,128)(2,1)S(1)}, u32[]{:S(2)}, u32[]{:S(2)}) async-start(bf16[8,304,256]{2,1,0:T(8,128)(2,1)} %shard_map.137), calls=%async_computation | async-start | bytes 2490368 | tf_op jit(solution)/shard_map/all_to_all | solution.py:304
  14.3 18.1 %copy-start = (bf16[256,256]{1,0:T(8,128)(2,1)S(1)}, bf16[256,256]{1,0:T(8,128)(2,1)}, u32[]{:S(2)}) copy-start(bf16[256,256]{1,0:T(8,128)(2,1)} %x_ref.5) | copy-start | bytes 393220
  15.0 46.7 %copy-start.1 = (bf16[256,32]{0,1:T(8,128)(2,1)S(1)}, bf16[256,32]{0,1:T(8,128)(2,1)}, u32[]{:S(2)}) copy-start(bf16[256,32]{0,1:T(8,128)(2,1)} %param.19) | copy-start | bytes 49156
  15.0 46.7 %copy-start.2 = (bf16[256,32]{0,1:T(8,128)(2,1)S(1)}, bf16[256,32]{0,1:T(8,128)(2,1)}, u32[]{:S(2)}) copy-start(bf16[256,32]{0,1:T(8,128)(2,1)} %param.13) | copy-start | bytes 49156
  126.8 8.8 %all-to-all-start.4 = ((bf16[8,3,8,128]{3,2,1,0:T(8,128)(2,1)}), bf16[8,3,8,128]{3,2,1,0:T(8,128)(2,1)S(1)}, u32[]{:S(2)}, u32[]{:S(2)}) async-start(bf16[8,3,8,128]{3,2,1,0:T(8,128)(2,1)} %get-tuple-element.24), calls=%async_computation.5 | async-start | bytes 98304 | tf_op jit(solution)/shard_map/all_to_all | solution.py:353
  136.8 39.4 %all-to-all-start.5 = ((bf16[64,9,8,128]{3,2,1,0:T(8,128)(2,1)}), bf16[64,9,8,128]{3,2,1,0:T(8,128)(2,1)S(1)}, u32[]{:S(2)}, u32[]{:S(2)}) async-start(bf16[64,9,8,128]{3,2,1,0:T(8,128)(2,1)} %shard_map.142), calls=%async_computation.6 | async-start | bytes 2359296 | tf_op jit(solution)/shard_map/all_to_all | solution.py:356
  144.7 39.3 %reduce-scatter.2.cloned.1.call-start = ((), (), s32[]{:S(2)}) async-start(), calls=%async_computation.7 | async-start | bytes 294912 | tf_op jit(solution)/shard_map/reduce_scatter | solution.py:346
Sparse Core Ops, SparseCore 0:
  148.9 35.0 reduce-scatter.1

commit v7 on v5

--- a/solution.py
+++ b/solution.py
@@ -39,8 +39,8 @@
 
 
 def hot(rows, index):
-    place = lax.broadcasted_iota(jnp.int32, (rows, index.shape[1]), 0)
-    return jnp.where(place == index, 1.0, 0.0).astype(BF16)
+    place = lax.broadcasted_iota(jnp.int16, (rows, index.shape[1]), 0)
+    return jnp.where(place == index.astype(jnp.int16), jnp.bfloat16(1), jnp.bfloat16(0))
 
 
 def call(kernel, out_shape, scratch=(), flops=0, vmem=16, places="", out_places=""):
@@ -255,40 +255,42 @@
         out_ref[n] = chunk
 
 
-def copy_kernel(got_ref, out_ref):
-    for n in range(SIDE):
-        for m in range(SIDE):
-            out_ref[n, m] = got_ref[m]
-
-
-def finish_kernel(core_ref, got_ref, basis_hbm, coef_ref, self_ref, basis_ref, rel_ref, own_ref, sems):
-    core = core_ref[0]
-    copies = []
-    for h in range(2):
-        place = pl.ds(h * 4, 4)
-        copies.append(pltpu.make_async_copy(basis_ref.at[place], basis_hbm.at[place], sems.at[h]))
-    for n in range(NE):
-        z, y = divmod(n, SIDE)
-        h, ib = divmod(n, 32)
-        part = got_ref[n + core * (y * SIDE + z - n)].astype(F32)
-        for l in range(4):
-            for o in range(2):
-                basis_ref[h * 4 + l, ib * 8 : ib * 8 + 8, o * 128 : o * 128 + 128] = part[l * 2 + o]
-        if n < 58:
-            for t in range(3):
-                piece = part[8] if t == 0 else pltpu.roll(part[8], 128 - 8 * t, 1)
-                rel_ref[n * REL_CHUNK + t * 8 : n * REL_CHUNK + t * 8 + 8, :] = piece
-        if n < 32:
-            own_ref[n * 8 : n * 8 + 8, :] = pltpu.roll(part[8], 96, 1)
-        if ib == 31:
-            copies[h].start()
+def copy_kernel(got_ref, out_hbm, sems):
+    copies = [pltpu.make_async_copy(got_ref, out_hbm.at[n], sems.at[n]) for n in range(SIDE)]
+    for copy in copies:
+        copy.start()
+    for copy in copies:
+        copy.wait()
+
+
+def finish_kernel(core_ref, got_ref, basis_ref, coef_ref, self_ref, rel_ref, own_ref):
+    def spread(place):
+        for n in range(NE):
+            h, ib = divmod(n, 32)
+            part = got_ref[place(*divmod(n, SIDE))].astype(F32)
+            for l in range(4):
+                for o in range(2):
+                    basis_ref[h * 4 + l, ib * 8 : ib * 8 + 8, o * 128 : o * 128 + 128] = part[l * 2 + o]
+            if n < 58:
+                for t in range(3):
+                    piece = part[8] if t == 0 else pltpu.roll(part[8], 128 - 8 * t, 1)
+                    rel_ref[n * REL_CHUNK + t * 8 : n * REL_CHUNK + t * 8 + 8, :] = piece
+            if n < 32:
+                own_ref[n * 8 : n * 8 + 8, :] = pltpu.roll(part[8], 96, 1)
+
+    @pl.when(core_ref[0] == 0)
+    def _():
+        spread(lambda z, y: z * SIDE + y)
+
+    @pl.when(core_ref[0] == 1)
+    def _():
+        spread(lambda z, y: y * SIDE + z)
+
     for t in range(11):
         across = rel_ref[t * 128 : (t + 1) * 128, :].T[0:8, :]
         width = min(128, RELS - t * 128)
         coef_ref[:, t * 128 : t * 128 + width] = across[:, 0:width]
     self_ref[...] = own_ref[...].T[0:32, :]
-    for copy in copies:
-        copy.wait()
 
 
 def lines(first):
@@ -397,20 +399,19 @@
         places="s",
     )(me, chunk, own)
     line = line_exchange(merged, 0)
-    copied = call(copy_kernel, shape((SIDE, SIDE, F_TILES, 8, 128), BF16))(line)
+    copied = call(
+        copy_kernel,
+        shape((SIDE, SIDE, F_TILES, 8, 128), BF16),
+        [pltpu.SemaphoreType.DMA((SIDE,))],
+        out_places="h",
+    )(line)
     gathered = line_exchange(copied, 1).reshape(NE, F_TILES, 8, 128)
 
     basis_grad, coef_t, self_grad_t = call(
         finish_kernel,
         (shape((GB, 256, 256), F32), shape((GB, RELS), F32), shape((COL, 256), F32)),
-        [
-            pltpu.VMEM((GB, 256, 256), F32),
-            pltpu.VMEM((11 * 128, 128), F32),
-            pltpu.VMEM((256, 128), F32),
-            pltpu.SemaphoreType.DMA((2,)),
-        ],
+        [pltpu.VMEM((11 * 128, 128), F32), pltpu.VMEM((256, 128), F32)],
         places="s",
-        out_places="h",
     )(lax.rem(me, 2), gathered)
     return (layer_t.T, input_grad_t.T, coef_t.T, basis_grad, self_grad_t.T)
 

time: 173 us -> 172 us (level)
  no operation moved by 1% of the time
where the time goes in v7:
time: 172 us; the launch traced here: 169 us
  blocking collectives  92.3 us (54%)
  waiting for transfers between devices  44.2 us (26%)
  Pallas kernels  19.2 us (11%)
  starting transfers between devices  11.4 us (7%)
    all_to_all x1, blocking collectives, body(): lax.all_to_all(terms, 'ent', split_axis=0, concat_axis=0, tiled=True)  38.3 us
    all_to_all x1, blocking collectives, body(): lax.all_to_all(message.reshape(NE, 8, 128), 'ent', split_axis=0, concat_a...  25.6 us
    all_to_all x1, waiting for transfers between devices, line_exchange(): lax.all_to_all(a, ('ent', 'rel'), split_axis=0, concat_axis=0, axis_index...  20.3 us
    pallas_call x8, Pallas kernels, run(): pl.pallas_call(kernel, out_shape=outs, in_specs=[spec(places, n) for n in...  19.2 us
    all_to_all x1, waiting for transfers between devices, body(): lax.all_to_all(payload, 'rel', split_axis=0, concat_axis=0, tiled=True)  17.3 us
    all_to_all x1, blocking collectives, body(): lax.all_to_all(back.reshape(NE, 8, 128), 'ent', split_axis=0, concat_axis...  16.7 us
    all_to_all x1, blocking collectives, line_exchange(): lax.all_to_all(a, ('ent', 'rel'), split_axis=0, concat_axis=0, axis_index...  11.8 us
    all_to_all x1, waiting for transfers between devices, body(): lax.all_to_all(chunk, 'rel', split_axis=0, concat_axis=0, tiled=True)  6.58 us
  transfers between devices with their start and end apart: 3, of which 3 were waited for; matrix products, arithmetic and copies ran while one was open for 0% of the time, Pallas kernels for 0%

profile of v7, /device:TPU:56, one launch (start us, length us, event | category | flops | bytes accessed | tf_op | source)
XLA Modules:
  0.0 168.6 jit_solution(14463010692890043565)
XLA Ops:
  0.6 2.6 %shard_map.137 = bf16[8,304,256]{2,1,0:T(8,128)(2,1)} custom-call(bf16[8,256,256]{2,1,0:T(8,128)(2,1)} %basis_ref.1, f32[8,1300]{1,0:T(8,128)} %bitcast.35), custom_call_target="tpu_custom_call" | custom-call | bytes 4194304 | tf_op jit(solution)/shard_map/pallas_call | solution.py:54
  3.2 0.0 copy-start.5
  3.3 0.0 copy-start.6
  3.3 4.4 %all-to-all-start = ((bf16[8,304,256]{2,1,0:T(8,128)(2,1)}), bf16[8,304,256]{2,1,0:T(8,128)(2,1)S(1)}, u32[]{:S(2)}, u32[]{:S(2)}) async-start(bf16[8,304,256]{2,1,0:T(8,128)(2,1)} %shard_map.137), calls=%async_computation | async-start | bytes 2490368 | tf_op jit(solution)/shard_map/all_to_all | solution.py:346
  7.8 0.2 copy.23
  8.0 0.2 reshape.44.index_ref
  8.2 0.1 copy.24
  8.3 0.1 reshape.45.weight_ref
  8.5 17.3 %all-to-all-done.w_ref = bf16[8,304,256]{2,1,0:T(8,128)(2,1)S(1)} async-done(((bf16[8,304,256]{2,1,0:T(8,128)(2,1)}), bf16[8,304,256]{2,1,0:T(8,128)(2,1)S(1)}, u32[]{:S(2)}, u32[]{:S(2)}) %all-to-all-start) | async-done | bytes 1245216 | tf_op jit(solution)/shard_map/all_to_all | solution.py:346
  25.8 3.8 %shard_map.138 = (bf16[512,128]{1,0:T(8,128)(2,1)S(1)}, f32[64,2048]{1,0:T(8,128)S(1)}) custom-call(bf16[8,304,256]{2,1,0:T(8,128)(2,1)S(1)} %all-to-all-done.w_ref, bf16[256,256]{1,0:T(8,128)(2,1)S(1)} %copy-done, s32[3,2048]{1,0:T(4,128)S(1)} %reshape.44.index_ref, f32[1,2048]{1,0:T(1,128)S(1)} %reshape.45.weight_ref), custom_call_target="tpu_custom_call" | custom-call | flops 5000000000 | bytes 4194304 | tf_op jit(solution)/shard_map/pallas_call | solution.py:54
  29.6 25.6 %all_to_all.35 = bf16[64,8,128]{2,1,0:T(8,128)(2,1)S(1)} all-to-all(bf16[64,8,128]{2,1,0:T(8,128)(2,1)S(1)} %bitcast.30), channel_id=1, replica_groups=mesh['ent'=64,'rel'=8] {'ent'}, dimensions={0} | all-to-all | bytes 262144 | tf_op jit(solution)/shard_map/all_to_all | solution.py:362
  55.2 1.4 shard_map.139
  56.5 16.7 %all_to_all.36 = bf16[64,8,128]{2,1,0:T(8,128)(2,1)S(1)} all-to-all(bf16[64,8,128]{2,1,0:T(8,128)(2,1)S(1)} %bitcast.29), channel_id=1, replica_groups=mesh['ent'=64,'rel'=8] {'ent'}, dimensions={0} | all-to-all | bytes 262144 | tf_op jit(solution)/shard_map/all_to_all | solution.py:370
  73.2 7.3 %shard_map.140 = (bf16[64,10,8,128]{3,2,1,0:T(8,128)(2,1)S(1)}, bf16[256,256]{1,0:T(8,128)(2,1)S(1)}) custom-call(bf16[512,128]{1,0:T(8,128)(2,1)S(1)} %bitcast.27, bf16[8,304,256]{2,1,0:T(8,128)(2,1)S(1)} %all-to-all-done.w_ref, f32[64,2048]{1,0:T(8,128)S(1)} %get-tuple-element.22.coef_ref, bf16[256,256]{1,0:T(8,128)(2,1)S(1)} %copy-done, ...), custom_call_target="tpu_custom_call" | custom-call | flops 8000000000 | bytes 4194304 | tf_op jit(solution)/shard_map/pallas_call | solution.py:54
  80.5 38.3 %all_to_all.37.got_ref = bf16[64,10,8,128]{3,2,1,0:T(8,128)(2,1)S(1)} all-to-all(bf16[64,10,8,128]{3,2,1,0:T(8,128)(2,1)S(1)} %get-tuple-element.24), channel_id=1, replica_groups=mesh['ent'=64,'rel'=8] {'ent'}, dimensions={0} | all-to-all | bytes 2621440 | tf_op jit(solution)/shard_map/all_to_all | solution.py:388
  118.8 0.9 shard_map.141
  119.7 3.4 %all-to-all-start.4 = ((bf16[8,11,8,128]{3,2,1,0:T(8,128)(2,1)}), bf16[8,11,8,128]{3,2,1,0:T(8,128)(2,1)S(1)}, u32[]{:S(2)}, u32[]{:S(2)}) async-start(bf16[8,11,8,128]{3,2,1,0:T(8,128)(2,1)} %get-tuple-element.26), calls=%async_computation.4 | async-start | bytes 360448 | tf_op jit(solution)/shard_map/all_to_all | solution.py:394
  123.1 6.6 %all-to-all-done.4.got_ref = bf16[8,11,8,128]{3,2,1,0:T(8,128)(2,1)S(1)} async-done(((bf16[8,11,8,128]{3,2,1,0:T(8,128)(2,1)}), bf16[8,11,8,128]{3,2,1,0:T(8,128)(2,1)S(1)}, u32[]{:S(2)}, u32[]{:S(2)}) %all-to-all-start.4) | async-done | bytes 180256 | tf_op jit(solution)/shard_map/all_to_all | solution.py:394
  129.7 0.6 shard_map.142
  130.3 11.8 %all_to_all.38.got_ref = bf16[8,9,8,128]{3,2,1,0:T(8,128)(2,1)S(1)} all-to-all(bf16[8,9,8,128]{3,2,1,0:T(8,128)(2,1)S(1)} %get-tuple-element.29), channel_id=1, replica_groups={{0,8,16,24,32,40,48,56},{64,72,80,88,96,104,112,120},{128,136,144,152,1..., dimensions={0} | all-to-all | bytes 294912 | tf_op jit(solution)/shard_map/all_to_all | solution.py:311
  142.1 1.1 shard_map.143
  143.2 3.6 %all-to-all-start.6 = ((bf16[8,8,9,8,128]{4,3,2,1,0:T(8,128)(2,1)}), bf16[8,8,9,8,128]{4,3,2,1,0:T(8,128)(2,1)S(1)}, u32[]{:S(2)}, u32[]{:S(2)}) async-start(bf16[8,8,9,8,128]{4,3,2,1,0:T(8,128)(2,1)} %shard_map.143), calls=%async_computation.6 | async-start | bytes 2359296 | tf_op jit(solution)/shard_map/all_to_all | solution.py:311
  146.7 20.3 %all-to-all-done.6 = bf16[8,8,9,8,128]{4,3,2,1,0:T(8,128)(2,1)S(1)} async-done(((bf16[8,8,9,8,128]{4,3,2,1,0:T(8,128)(2,1)}), bf16[8,8,9,8,128]{4,3,2,1,0:T(8,128)(2,1)S(1)}, u32[]{:S(2)}, u32[]{:S(2)}) %all-to-all-start.6) | async-done | bytes 1179680 | tf_op jit(solution)/shard_map/all_to_all | solution.py:311
  167.0 1.6 shard_map.144
  (16 shorter events, 0.1 us)
Async XLA Ops:
  3.2 4.5 %copy-start.4 = (s32[64,32]{0,1:T(8,128)S(1)}, s32[64,32]{0,1:T(8,128)}, u32[]{:S(2)}) copy-start(s32[64,32]{0,1:T(8,128)} %param.16) | copy-start | bytes 24580
  3.2 4.5 %copy-start.5 = (s32[64,32]{0,1:T(8,128)S(1)}, s32[64,32]{0,1:T(8,128)}, u32[]{:S(2)}) copy-start(s32[64,32]{0,1:T(8,128)} %param.15) | copy-start | bytes 24580
  3.3 4.5 %copy-start.6 = (s32[64,32]{0,1:T(8,128)S(1)}, s32[64,32]{0,1:T(8,128)}, u32[]{:S(2)}) copy-start(s32[64,32]{0,1:T(8,128)} %param.14) | copy-start | bytes 24580
  3.3 4.9 %copy-start.3 = (f32[64,32]{0,1:T(8,128)S(1)}, f32[64,32]{0,1:T(8,128)}, u32[]{:S(2)}) copy-start(f32[64,32]{0,1:T(8,128)} %param.17) | copy-start | bytes 24580
  3.3 4.9 %copy-start.7 = (s32[1,64]{1,0:T(1,128)S(1)}, s32[1,64]{1,0:T(1,128)}, u32[]{:S(2)}) copy-start(s32[1,64]{1,0:T(1,128)} %param.18) | copy-start | bytes 772
  3.3 22.5 %all-to-all-start = ((bf16[8,304,256]{2,1,0:T(8,128)(2,1)}), bf16[8,304,256]{2,1,0:T(8,128)(2,1)S(1)}, u32[]{:S(2)}, u32[]{:S(2)}) async-start(bf16[8,304,256]{2,1,0:T(8,128)(2,1)} %shard_map.137), calls=%async_computation | async-start | bytes 2490368 | tf_op jit(solution)/shard_map/all_to_all | solution.py:346
  7.7 18.1 %copy-start = (bf16[256,256]{1,0:T(8,128)(2,1)S(1)}, bf16[256,256]{1,0:T(8,128)(2,1)}, u32[]{:S(2)}) copy-start(bf16[256,256]{1,0:T(8,128)(2,1)} %x_ref.5) | copy-start | bytes 393220
  8.4 46.7 %copy-start.1 = (bf16[256,32]{0,1:T(8,128)(2,1)S(1)}, bf16[256,32]{0,1:T(8,128)(2,1)}, u32[]{:S(2)}) copy-start(bf16[256,32]{0,1:T(8,128)(2,1)} %param.19) | copy-start | bytes 49156
  8.5 46.7 %copy-start.2 = (bf16[256,32]{0,1:T(8,128)(2,1)S(1)}, bf16[256,32]{0,1:T(8,128)(2,1)}, u32[]{:S(2)}) copy-start(bf16[256,32]{0,1:T(8,128)(2,1)} %param.13) | copy-start | bytes 49156
  119.7 10.0 %all-to-all-start.4 = ((bf16[8,11,8,128]{3,2,1,0:T(8,128)(2,1)}), bf16[8,11,8,128]{3,2,1,0:T(8,128)(2,1)S(1)}, u32[]{:S(2)}, u32[]{:S(2)}) async-start(bf16[8,11,8,128]{3,2,1,0:T(8,128)(2,1)} %get-tuple-element.26), calls=%async_computation.4 | async-start | bytes 360448 | tf_op jit(solution)/shard_map/all_to_all | solution.py:394
  143.2 23.9 %all-to-all-start.6 = ((bf16[8,8,9,8,128]{4,3,2,1,0:T(8,128)(2,1)}), bf16[8,8,9,8,128]{4,3,2,1,0:T(8,128)(2,1)S(1)}, u32[]{:S(2)}, u32[]{:S(2)}) async-start(bf16[8,8,9,8,128]{4,3,2,1,0:T(8,128)(2,1)} %shard_map.143), calls=%async_computation.6 | async-start | bytes 2359296 | tf_op jit(solution)/shard_map/all_to_all | solution.py:311
